TPU v7x, 512 devices: a whole 4x8x8 slice. The times are simulated.
512 devices in a mesh: grp: 2 (over y_lo), tile: 64 (over x, z, core), tp: 4 (over y_hi).
Axes of the slice: x: 4, y: 8 (y_hi: 4, y_lo: 2; y = y_hi * 2 + y_lo), z: 8, core: 2. Of those that a mesh axis runs over, the one named last changes fastest.
Arguments:
- atmos_state: bfloat16 [65536, 1536], P(('grp', 'tile')), may hold values from -6 to 6
- atmos_gain: float32 [1536], replicated, may hold values from 0.25 to 1.75
- w_first: bfloat16 [1536, 3072], P(('grp', 'tile'), 'tp'), may hold values from -0.15625 to 0.15625
- w_second: bfloat16 [1536, 3072], P(('grp', 'tile'), 'tp'), may hold values from -0.109375 to 0.109375
- flux_proj: bfloat16 [1536, 256], replicated, may hold values from -0.15625 to 0.15625
- remap_index: int32 [1024, 3], P(('grp', 'tile', 'tp')), may hold values from 0 to 3
- remap_weight: bfloat16 [1024, 3, 128, 128], P(('grp', 'tile', 'tp')), may hold values from -0.3125 to 0.3125
- ocean_state: bfloat16 [1024, 128, 256], P(('grp', 'tile'), 'tp'), may hold values from -6 to 6
- depth_levels: int32 [1024, 128], P(('grp', 'tile'), 'tp'), may hold values from 0 to 16
- conv_kernel: float32 [3, 3, 256], replicated, may hold values from -2 to 2
- ocean_gain: float32 [256], replicated, may hold values from 0.25 to 1.75
- ocean_w_in: bfloat16 [256, 1024], replicated, may hold values from -0.375 to 0.375
- ocean_w_out: bfloat16 [1024, 256], replicated, may hold values from -0.1875 to 0.1875
- ocean_cotangent: bfloat16 [1024, 128, 256], P(('grp', 'tile'), 'tp'), may hold values from -6 to 6
Outputs:
- atmos_out: bfloat16 [65536, 1536], P(('grp', 'tile', 'tp'))
- ocean_out: bfloat16 [1024, 128, 256], P(('grp', 'tile'), 'tp')
- weight_grads: float32 [2048, 256], P(('grp', 'tile', 'tp'))
Inputs may be any that keep to these rules, and one draw needn't show every extreme that they name: `remap_index`: index the 128-token blocks among the 512 atmosphere tokens of the same grp and tile indices as the ocean tile of that block. `depth_levels`: 0 marks land.
All inputs are finite; a program needn't handle non-finite values.
Results may differ from a plain program's by a relative error of at most 0.018.
Values may be sent and summed in bfloat16 or wider, within the bound.
A program may use at most 64 MiB of HBM per device.

v0:
```python
import jax
import jax.numpy as jnp
from jax import lax
from jax.sharding import PartitionSpec as P

LEV = 16


epsilon = 1e-06


def with_halo(block, sides, width):
    for axis, dim in sides:
        count = lax.axis_size(axis)
        forward = [(i, i + 1) for i in range(count - 1)]
        backward = [(target, source) for source, target in forward]
        low = lax.ppermute(
            lax.slice_in_dim(block, block.shape[dim] - width, None, axis=dim), axis, forward
        )
        high = lax.ppermute(lax.slice_in_dim(block, 0, width, axis=dim), axis, backward)
        block = jnp.concatenate([low, block, high], axis=dim)
    return block


def rms_norm(values, gain):
    wide = values.astype(jnp.float32)
    scale = lax.rsqrt(jnp.mean(wide * wide, axis=-1, keepdims=True) + epsilon)
    return (wide * scale * gain).astype(jnp.bfloat16)


def on_device(
    atmos_state,
    atmos_gain,
    w_first,
    w_second,
    flux_proj,
    remap_index,
    remap_weight,
    ocean_state,
    depth_levels,
    conv_kernel,
    ocean_gain,
    ocean_w_in,
    ocean_w_out,
    ocean_cotangent,
):
    normed = rms_norm(atmos_state, atmos_gain)
    rows_all = atmos_state.shape[0]
    hsum = jnp.dot(
        normed,
        lax.all_gather(w_first, ("grp", "tile"), axis=0, tiled=True),
        preferred_element_type=jnp.float32,
    )
    hidden = jax.nn.gelu(hsum).astype(jnp.bfloat16)
    partial_sum = lax.dot_general(
        hidden,
        lax.all_gather(w_second, ("grp", "tile"), axis=0, tiled=True),
        (((1,), (1,)), ((), ())),
        preferred_element_type=jnp.float32,
    )
    rows_own = rows_all // lax.axis_size("tp")
    block_rows = remap_weight.shape[2]
    channels = flux_proj.shape[1]
    summed = lax.psum_scatter(
        partial_sum.astype(jnp.bfloat16), "tp", scatter_dimension=0, tiled=True
    ).astype(jnp.float32)
    own_rows = lax.dynamic_slice_in_dim(atmos_state, lax.axis_index("tp") * rows_own, rows_own, 0)
    atmos_out = (own_rows.astype(jnp.float32) + summed).astype(jnp.bfloat16)
    flux = jnp.dot(atmos_out, flux_proj, preferred_element_type=jnp.float32).astype(jnp.bfloat16)
    piece = lax.all_gather(flux, "tp", axis=0, tiled=True)
    count = piece.shape[0] // block_rows
    blocks = piece.reshape(count, block_rows, channels)
    targets = jnp.arange(count, dtype=jnp.int32)
    select = (remap_index[:, :, None] == targets[None, None, :]).astype(jnp.bfloat16)
    picked = jnp.einsum("bkj,jrc->bkrc", select, blocks, preferred_element_type=jnp.float32).astype(
        jnp.bfloat16
    )
    remapped = jnp.einsum(
        "bksr,bkrc->bsc", remap_weight, picked, preferred_element_type=jnp.float32
    )
    tile_x, tile_y, _ = ocean_state.shape
    levels = jnp.arange(channels, dtype=jnp.int32) // (channels // LEV)
    wet = (levels[None, None, :] < depth_levels[:, :, None]).astype(jnp.float32)
    moved = remapped.astype(jnp.bfloat16).reshape(tile_x, tile_y, channels)
    field = ((ocean_state.astype(jnp.float32) + moved.astype(jnp.float32)) * wet).astype(
        jnp.bfloat16
    )
    padded = with_halo(field, ((("grp", "tile"), 0), ("tp", 1)), 1).astype(jnp.float32)
    conv = jnp.zeros((tile_x, tile_y, channels), jnp.float32)
    for i in range(3):
        for j in range(3):
            conv = conv + conv_kernel[i, j] * padded[i : i + tile_x, j : j + tile_y]
    centred = conv - jnp.mean(conv, axis=-1, keepdims=True)
    variance = jnp.mean(centred * centred, axis=-1, keepdims=True)
    cells = tile_x * tile_y
    ocean_normed = (
        (centred * lax.rsqrt(variance + epsilon) * ocean_gain)
        .astype(jnp.bfloat16)
        .reshape(cells, channels)
    )
    flat_field = field.reshape(cells, channels)
    flat_wet = wet.reshape(cells, channels)
    pre = jnp.dot(ocean_normed, ocean_w_in, preferred_element_type=jnp.float32)
    activated, backward = jax.vjp(jax.nn.gelu, pre)
    activated = activated.astype(jnp.bfloat16)
    out = jnp.dot(activated, ocean_w_out, preferred_element_type=jnp.float32)
    ocean_out = (
        ((flat_field.astype(jnp.float32) + out) * flat_wet)
        .astype(jnp.bfloat16)
        .reshape(tile_x, tile_y, channels)
    )
    dout = (ocean_cotangent.reshape(cells, channels).astype(jnp.float32) * flat_wet).astype(
        jnp.bfloat16
    )
    dact = lax.dot_general(
        dout, ocean_w_out, (((1,), (1,)), ((), ())), preferred_element_type=jnp.float32
    )
    dpre = backward(dact)[0].astype(jnp.bfloat16)
    grad_in = lax.dot_general(
        dpre, ocean_normed, (((0,), (0,)), ((), ())), preferred_element_type=jnp.float32
    )
    grad_out = lax.dot_general(
        activated, dout, (((0,), (0,)), ((), ())), preferred_element_type=jnp.float32
    )
    terms = jnp.concatenate([grad_in, grad_out], axis=0)
    weight_grads = lax.psum_scatter(terms, ("grp", "tile", "tp"), scatter_dimension=0, tiled=True)
    return (atmos_out, ocean_out, weight_grads)


def solution(mesh):
    in_specs = (
        P(("grp", "tile"), None),
        P(),
        P(("grp", "tile"), "tp"),
        P(("grp", "tile"), "tp"),
        P(),
        P(("grp", "tile", "tp"), None),
        P(("grp", "tile", "tp"), None, None, None),
        P(("grp", "tile"), "tp", None),
        P(("grp", "tile"), "tp"),
        P(),
        P(),
        P(),
        P(),
        P(("grp", "tile"), "tp", None),
    )
    out_specs = (
        P(("grp", "tile", "tp"), None),
        P(("grp", "tile"), "tp", None),
        P(("grp", "tile", "tp"), None),
    )
    return jax.shard_map(
        on_device, mesh=mesh, in_specs=in_specs, out_specs=out_specs, check_vma=False
    )
```

profile of v0, /device:TPU:1, one launch (start us, length us, event | category | flops | bytes accessed | tf_op | source)
XLA Modules:
  0.0 840.9 jit_solution(13579727975106779312)
XLA Ops:
  7.2 0.0 copy-start
  7.2 0.0 all-gather.7.cloned.1.call-start
  7.2 0.7 all-gather.7.cloned.1.call-update
  7.9 0.0 all-gather.5.cloned.1.call-start
  8.0 0.7 all-gather.5.cloned.1.call-update
  8.7 0.0 reduce-scatter.2.cloned.1.call-start
  8.7 1.8 fusion
  10.5 223.0 %all-gather.7.cloned.1.call-done = bf16[128,12,768]{2,1,0:T(8,128)(2,1)} async-done(((bf16[1,12,768]{2,1,0:T(8,128)(2,1)}), bf16[128,12,768]{2,1,0:T(8,128)(2,1)}) %all-gather.7.cloned.1.call-update) | async-done | bytes 2359312 | tf_op jit(solution)/shard_map/all_gather | solution.py:57
  233.5 5.0 reshape.72
  238.5 0.0 copy-start.1
  238.5 0.0 copy-start.12
  238.5 214.5 %all-gather.5.cloned.1.call-done = bf16[128,12,768]{2,1,0:T(8,128)(2,1)} async-done(((bf16[1,12,768]{2,1,0:T(8,128)(2,1)}), bf16[128,12,768]{2,1,0:T(8,128)(2,1)}) %all-gather.5.cloned.1.call-update) | async-done | bytes 2359312 | tf_op jit(solution)/shard_map/all_gather | solution.py:51
  453.0 5.0 reshape.70
  458.0 0.0 copy-done.1
  458.0 0.0 copy-done.12
  458.0 6.8 convolution_convert_fusion
  464.8 0.0 reduce-scatter.2.cloned.1.call-update
  464.8 0.0 copy-start.4
  464.8 0.0 all-reduce.3.cloned.1.call-start
  464.9 0.0 copy-done.7
  464.9 0.1 lt.27
  465.0 43.7 %reduce-scatter.2.cloned.1.call-done = bf16[128,1536]{1,0:T(8,128)(2,1)} async-done(((bf16[512,1536]{1,0:T(8,128)(2,1)}), bf16[128,1536]{1,0:T(8,128)(2,1)}) %reduce-scatter.2.cloned.1.call-update) | async-done | bytes 393232 | tf_op jit(solution)/shard_map/reduce_scatter | solution.py:64
  508.7 1.1 add_convert_fusion
  509.8 0.0 copy-done
  509.8 0.0 copy-start.2
  509.8 0.0 copy-start.5
  509.9 0.0 copy-start.8
  509.9 0.3 convolution_convert_fusion.2
  510.1 11.5 %all_gather.11 = bf16[512,256]{1,0:T(8,128)(2,1)S(1)} all-gather(bf16[128,256]{1,0:T(8,128)(2,1)S(1)} %convolution_convert_fusion.2), channel_id=1, replica_groups=mesh['grp'=2,'tile'=64,'tp'=4] {'tp'}, dimensions={0}, use_global_device_ids=true | all-gather | bytes 327680 | tf_op jit(solution)/shard_map/all_gather | solution.py:70
  521.6 0.0 copy-done.9
  521.6 0.4 convolution_convert_fusion.1
  522.0 0.0 copy-done.4
  522.0 0.2 fusion.19
  522.2 0.0 copy-done.6
  522.2 0.1 select_convert_fusion
  522.4 0.0 copy-start.10
  522.4 5.3 collective-permute-start.1
  527.7 3.2 collective-permute-start
  530.9 0.0 copy-done.5
  530.9 0.1 fusion.33
  531.0 0.0 copy-start.3
  531.0 0.0 collective-permute-done.1
  531.0 0.7 collective-permute-done
  531.8 0.0 copy-done.2
  531.8 1.3 collective-permute-start.3
  533.1 5.5 collective-permute-start.2
  538.6 0.0 copy-done.8
  538.6 0.0 collective-permute-done.3
  538.6 0.8 collective-permute-done.2
  539.4 0.1 maximum_convert_fusion
  539.4 0.3 fusion.58
  539.7 0.2 multiply_reduce_fusion
  539.9 0.0 copy-done.10
  539.9 0.1 multiply_convert_fusion.1
  540.1 0.0 copy-done.3
  540.1 0.3 fusion.64
  540.4 0.6 fusion.57
  541.0 3.1 fusion.30
  544.1 2.7 pad_maximum_fusion
  546.8 0.0 all-reduce.3.cloned.1.call-update
  546.8 1.0 copy-done.11
  547.8 1.1 fusion.20
  549.0 284.1 %all-reduce.3.cloned.1.call-done = f32[2048,256]{1,0:T(8,128)} async-done(((f32[2048,256]{1,0:T(8,128)}), f32[2048,256]{1,0:T(8,128)}) %all-reduce.3.cloned.1.call-update) | async-done | bytes 2097168
  833.1 1.3 constant_dynamic-slice_fusion
  (11 shorter events, 0.1 us)
Async XLA Ops:
  7.2 502.7 %copy-start = (bf16[1536,256]{1,0:T(8,128)(2,1)S(1)}, bf16[1536,256]{1,0:T(8,128)(2,1)}, u32[]{:S(2)}) copy-start(bf16[1536,256]{1,0:T(8,128)(2,1)} %param.18) | copy-start | bytes 2359300
  7.2 226.3 %all-gather.7.cloned.1.call-start = ((), (), s32[]{:S(2)}) async-start(), calls=%async_computation.3 | async-start | bytes 3170304 | tf_op jit(solution)/shard_map/all_gather | solution.py:57
  7.9 445.1 %all-gather.5.cloned.1.call-start = ((), (), s32[]{:S(2)}) async-start(), calls=%async_computation.2 | async-start | bytes 3170304 | tf_op jit(solution)/shard_map/all_gather | solution.py:51
  8.7 500.1 %reduce-scatter.2.cloned.1.call-start = ((), (), s32[]{:S(2)}) async-start(), calls=%async_computation.1 | async-start | bytes 1966080 | tf_op jit(solution)/shard_map/reduce_scatter | solution.py:64
  238.5 219.5 %copy-start.1 = (bf16[512,1536]{1,0:T(8,128)(2,1)S(1)}, bf16[512,1536]{1,0:T(8,128)(2,1)}, u32[]{:S(2)}) copy-start(bf16[512,1536]{1,0:T(8,128)(2,1)} %param.14) | copy-start | bytes 4718596
  238.5 219.5 %copy-start.12 = (f32[1536]{0:T(1024)S(1)}, f32[1536]{0:T(1024)}, u32[]{:S(2)}) copy-start(f32[1536]{0:T(1024)} %param.15) | copy-start | bytes 18436
  458.0 6.9 copy-start.7
  464.8 56.8 %copy-start.9 = (s32[2,3]{1,0:T(2,128)S(1)}, s32[2,3]{1,0:T(2,128)}, u32[]{:S(2)}) copy-start(s32[2,3]{1,0:T(2,128)} %param.19) | copy-start | bytes 76
  464.8 57.2 %copy-start.4 = (bf16[2,3,128,128]{3,2,1,0:T(8,128)(2,1)S(1)}, bf16[2,3,128,128]{3,2,1,0:T(8,128)(2,1)}, u32[]{:S(2)}) copy-start(bf16[2,3,128,128]{3,2,1,0:T(8,128)(2,1)} %param.20) | copy-start | bytes 589828
  464.8 368.2 %all-reduce.3.cloned.1.call-start = ((), (), s32[]{:S(2)}) async-start(), calls=%async_computation.4 | async-start | bytes 4194304
  465.0 57.3 %copy-start.6 = (bf16[8,32,256]{2,1,0:T(8,128)(2,1)S(1)}, bf16[8,32,256]{2,1,0:T(8,128)(2,1)}, u32[]{:S(2)}) copy-start(bf16[8,32,256]{2,1,0:T(8,128)(2,1)} %param.21) | copy-start | bytes 393220
  509.8 21.9 %copy-start.2 = (bf16[128,1536]{1,0:T(8,128)(2,1)}, bf16[128,1536]{1,0:T(8,128)(2,1)S(1)}, u32[]{:S(2)}) copy-start(bf16[128,1536]{1,0:T(8,128)(2,1)S(1)} %add_convert_fusion) | copy-start | bytes 1179652
  509.8 21.1 %copy-start.5 = (bf16[8,32,256]{2,1,0:T(8,128)(2,1)S(1)}, bf16[8,32,256]{2,1,0:T(8,128)(2,1)}, u32[]{:S(2)}) copy-start(bf16[8,32,256]{2,1,0:T(8,128)(2,1)} %param.27) | copy-start | bytes 393220
  509.9 28.7 %copy-start.8 = (f32[3,3,256]{2,1,0:T(4,128)S(1)}, f32[3,3,256]{2,1,0:T(4,128)}, u32[]{:S(2)}) copy-start(f32[3,3,256]{2,1,0:T(4,128)} %param.23) | copy-start | bytes 27652
  522.4 17.6 %copy-start.10 = (f32[256]{0:T(256)S(1)}, f32[256]{0:T(256)}, u32[]{:S(2)}) copy-start(f32[256]{0:T(256)} %param.24) | copy-start | bytes 3076
  522.4 8.7 %collective-permute-start.1 = (bf16[1,32,256]{2,1,0:T(8,128)(2,1)S(1)}, bf16[1,32,256]{2,1,0:T(8,128)(2,1)S(1)}, u32[]{:S(2)}, u32[]{:S(2)}) collective-permute-start(bf16[1,32,256]{2,1,0:T(8,128)(2,1)S(1)} %get-tuple-element.8), channel_id=1, source_target_pairs={{4,0},{8,4},{12,8},{16,12},{20,16},{24,20},{28,24},{32,28},{36,32}... | collective-permute-start | bytes 49160 | tf_op jit(solution)/shard_map/ppermute | solution.py:20
  527.7 4.0 collective-permute-start
  531.0 9.1 %copy-start.3 = (bf16[256,1024]{1,0:T(8,128)(2,1)S(1)}, bf16[256,1024]{1,0:T(8,128)(2,1)}, u32[]{:S(2)}) copy-start(bf16[256,1024]{1,0:T(8,128)(2,1)} %param.25) | copy-start | bytes 1572868
  531.8 6.8 collective-permute-start.3
  533.1 6.3 collective-permute-start.2
  546.8 1.0 copy-start.11
Sparse Core Ops, SparseCore 0:
  10.2 223.2 all-gather.6
  235.7 217.3 all-gather.4
  464.9 43.7 reduce-scatter.1
  546.9 286.0 all-reduce.2
where the time goes:
time: 842 us; the launch traced here: 841 us
  waiting for transfers between devices  768 us (91%)
  starting transfers between devices  15.4 us (2%)
  between operations  14.1 us (2%)
  matrix products  12.8 us (2%)
  local copies, waits for them, and re-layouts  12.4 us (1%)
  blocking collectives  11.5 us (1%)
    unnamed x5, waiting for transfers between devices  286 us
    all_gather x1, waiting for transfers between devices, on_device(): lax.all_gather(w_second, ('grp', 'tile'), axis=0, tiled=True)  223 us
    all_gather x1, waiting for transfers between devices, on_device(): lax.all_gather(w_first, ('grp', 'tile'), axis=0, tiled=True)  215 us
    reduce_scatter x1, waiting for transfers between devices, on_device(): lax.psum_scatter(partial_sum.astype(jnp.bfloat16), 'tp', scatter_dimensio...  43.7 us
  transfers between devices with their start and end apart: 8, of which 6 were waited for; matrix products, arithmetic and copies ran while one was open for 1% of the time, Pallas kernels for 0%

commit v1 on v0

--- a/solution.py
+++ b/solution.py
@@ -1,12 +1,466 @@
 import jax
 import jax.numpy as jnp
 from jax import lax
+from jax.experimental import pallas as pl
+from jax.experimental.pallas import tpu as pltpu
 from jax.sharding import PartitionSpec as P
 
 LEV = 16
-
-
+MESH = pl.DeviceIdType.MESH
 epsilon = 1e-06
+
+
+def coords():
+    g = lax.axis_index("grp")
+    t = lax.axis_index("tile")
+    p = lax.axis_index("tp")
+    return t // 16, p * 2 + g, (t // 2) % 8, t % 2
+
+
+def device_at(x, y, z, c):
+    return (y % 2, x * 16 + z * 2 + c, y // 2)
+
+
+def peer(dx=0, dy=0, dz=0, dc=0):
+    x, y, z, c = coords()
+    return device_at((x + dx) % 4, (y + dy) % 8, (z + dz) % 8, (c + dc) % 2)
+
+
+def barrier(peers):
+    sem = pltpu.get_barrier_semaphore()
+    for dev in peers:
+        pl.semaphore_signal(sem, inc=1, device_id=dev, device_id_type=MESH)
+    pl.semaphore_wait(sem, len(peers))
+
+
+class Comm:
+    def __init__(self, send_sems, recv_sems):
+        self.send_sems = send_sems
+        self.recv_sems = recv_sems
+        self.count = 0
+        self.sent = []
+
+    def send(self, src, dst, dev):
+        k = self.count
+        self.count += 1
+        copy = pltpu.make_async_remote_copy(
+            src_ref=src,
+            dst_ref=dst,
+            send_sem=self.send_sems.at[k],
+            recv_sem=self.recv_sems.at[k],
+            device_id=dev,
+            device_id_type=MESH,
+        )
+        copy.start()
+        self.sent.append(copy)
+        return k
+
+    def recv(self, k, ref):
+        pltpu.make_async_remote_copy(
+            src_ref=ref,
+            dst_ref=ref,
+            send_sem=self.send_sems.at[k],
+            recv_sem=self.recv_sems.at[k],
+            device_id=peer(dc=1),
+            device_id_type=MESH,
+        ).wait_recv()
+
+    def drain(self):
+        for copy in self.sent:
+            copy.wait_send()
+        self.sent = []
+
+
+def gelu(v):
+    return 0.5 * v * (1.0 + jnp.tanh(0.7978845608028654 * (v + 0.044715 * (v * v * v))))
+
+
+def atmos_peers():
+    x, y, z, c = coords()
+    g = y % 2
+    y_pair = y + 1 - 2 * g
+    out = [peer(dc=1), device_at(x, y_pair, z, c), device_at(x, y_pair, z, 1 - c)]
+    out += [peer(dx=i) for i in (1, 2, 3)]
+    out += [peer(dz=1), peer(dz=7)]
+    out += [peer(dy=i) for i in (2, 4, 6)]
+    return out
+
+
+def atmos_kernel(
+    state, gain, w1, w2, proj,
+    atmos_out, flux_all,
+    stage, compose, g1, g2, w1n, w2n, normed, hidden, part, fluxp, fluxin, partin,
+    send_sems, recv_sems,
+):
+    x, y, z, c = coords()
+    g = y % 2
+    p = y // 2
+    y_pair = y + 1 - 2 * g
+    comm = Comm(send_sems, recv_sems)
+    slot = 2 * g + c
+    stage[slot] = jnp.zeros(stage.shape[1:], stage.dtype)
+    stage[slot, 0, 0:12, :] = w1[...]
+    stage[slot, 1, 0:12, :] = w2[...]
+    barrier(atmos_peers())
+
+    own = stage.at[slot]
+    k_core = comm.send(own, own, device_at(x, y, z, 1 - c))
+    k_pair = comm.send(own, own, device_at(x, y_pair, z, c))
+    k_diag = comm.send(own, own, device_at(x, y_pair, z, 1 - c))
+
+    rows = 64
+
+    @pl.loop(0, state.shape[0] // rows)
+    def _(i):
+        at = pl.ds(pl.multiple_of(i * rows, rows), rows)
+        wide = state[at, :].astype(jnp.float32)
+        scale = lax.rsqrt(jnp.mean(wide * wide, axis=-1, keepdims=True) + epsilon)
+        normed[at, :] = (wide * scale * gain[...]).astype(jnp.bfloat16)
+
+    comm.recv(k_core, stage.at[2 * g + 1 - c])
+    comm.recv(k_pair, stage.at[2 * (1 - g) + c])
+    comm.recv(k_diag, stage.at[2 * (1 - g) + 1 - c])
+    for w, dest in ((0, g1), (1, g2)):
+        for s in range(4):
+            compose[w, 12 * s : 12 * s + 12, :] = stage[s, w].astype(jnp.float32)[0:12, :]
+        dest[x, z] = compose[w].astype(jnp.bfloat16)
+
+    half = pl.ds(pl.multiple_of(c * 384, 128), 384)
+    other = pl.ds(pl.multiple_of((1 - c) * 384, 128), 384)
+
+    def xi(i):
+        return (x + i + 4) % 4
+
+    def zi(i):
+        return (z + i + 8) % 8
+
+    handed = []
+
+    def hand(buf, *index):
+        ref = buf.at[index[0], index[1], index[2], half]
+        k = comm.send(ref, ref, peer(dc=1))
+        handed.append((k, buf.at[index[0], index[1], index[2], other]))
+
+    every = pl.ds(0, 48)
+    low = pl.ds(0, 32)
+    high = pl.ds(32, 16)
+
+    k1x = {}
+    for i in (1, 3, 2):
+        ref = g1.at[x, z, every, half]
+        k1x[i] = comm.send(ref, ref, peer(dx=i))
+    k2z = {}
+    for d in (1, -1):
+        ref = g2.at[x, z, every, half]
+        k2z[1, d] = comm.send(ref, ref, peer(dz=d))
+    k2x = {}
+
+    def start_2x(j):
+        for d in (1, -1):
+            ref = g2.at[x, zi(j), every, half]
+            k2x[1, j, d] = comm.send(ref, ref, peer(dx=d))
+
+    start_2x(0)
+    k1z = {}
+
+    def start_1z(i):
+        for d in (1, -1):
+            ref = g1.at[xi(i), z, every, half]
+            k1z[1, i, d] = comm.send(ref, ref, peer(dz=d))
+
+    start_1z(0)
+    for i in (1, 3, 2):
+        comm.recv(k1x[i], g1.at[xi(-i), z, every, half])
+        start_1z(-i % 4)
+        hand(g1, xi(-i), z, every)
+
+    def round_2z(r):
+        for d in (1, -1):
+            at = zi(-r * d)
+            if r < 4:
+                comm.recv(k2z[r, d], g2.at[x, at, every, half])
+                if r < 3:
+                    piece = every
+                else:
+                    piece = low if d == 1 else high
+                ref = g2.at[x, at, piece, half]
+                k2z[r + 1, d] = comm.send(ref, ref, peer(dz=d))
+                start_2x(-r * d)
+                hand(g2, x, at, every)
+            else:
+                piece = low if d == 1 else high
+                comm.recv(k2z[r, d], g2.at[x, at, piece, half])
+                if d == -1:
+                    start_2x(4)
+                    hand(g2, x, at, every)
+
+    order_1 = (0, 3, 1, 2)
+
+    def round_1z(r, n):
+        i = order_1[n]
+        for d in (1, -1):
+            at = zi(-r * d)
+            if r == 4 and (n < 2) != (d == 1):
+                continue
+            comm.recv(k1z[r, i, d], g1.at[xi(i), at, every, half])
+            if r < 3 or (r == 3 and (n < 2) == (d == 1)):
+                ref = g1.at[xi(i), at, every, half]
+                k1z[r + 1, i, d] = comm.send(ref, ref, peer(dz=d))
+            hand(g1, xi(i), at, every)
+
+    order_2 = (0, -1, 1, -2, 2, -3, 3, 4)
+
+    def round_2x(r, n):
+        j = order_2[n]
+        for d in (1, -1):
+            at = xi(-r * d)
+            if r == 2 and (n < 4) != (d == 1):
+                continue
+            comm.recv(k2x[r, j, d], g2.at[at, zi(j), every, half])
+            if r == 1 and (n < 4) == (d == 1):
+                ref = g2.at[at, zi(j), every, half]
+                k2x[2, j, d] = comm.send(ref, ref, peer(dx=d))
+            hand(g2, at, zi(j), every)
+
+    round_2z(1)
+    round_1z(1, 0)
+    round_2z(2)
+    round_2x(1, 0)
+    round_1z(1, 1)
+    round_2z(3)
+    round_1z(1, 2)
+    round_2x(1, 1)
+    round_2z(4)
+    round_1z(1, 3)
+    later_2x = [(1, n) for n in range(2, 8)] + [(2, n) for n in range(8)]
+    later_1z = [(2, n) for n in range(4)] + [(3, n) for n in range(4)] + [(4, n) for n in range(4)]
+    while later_1z or later_2x:
+        if later_2x:
+            round_2x(*later_2x.pop(0))
+        if later_1z:
+            round_1z(*later_1z.pop(0))
+    for k, ref in handed:
+        comm.recv(k, ref)
+
+    for src, dst in ((g1, w1n), (g2, w2n)):
+
+        @pl.loop(0, 16)
+        def _(j):
+            a = src[j // 4, 2 * (j % 4)].astype(jnp.float32)
+            b = src[j // 4, 2 * (j % 4) + 1].astype(jnp.float32)
+            at = pl.multiple_of(j * 48, 16)
+            dst[pl.ds(at, 48), :] = jnp.concatenate([a[:24], b[:24]], axis=0).astype(jnp.bfloat16)
+            dst[pl.ds(768 + at, 48), :] = jnp.concatenate([a[24:], b[24:]], axis=0).astype(jnp.bfloat16)
+
+    @pl.loop(0, 3)
+    def _(n):
+        at = pl.ds(pl.multiple_of(n * 256, 256), 256)
+        pre = jnp.dot(normed[...], w1n[:, at], preferred_element_type=jnp.float32)
+        hidden[:, at] = gelu(pre).astype(jnp.bfloat16)
+
+    fluxp[...] = jnp.zeros(fluxp.shape, jnp.float32)
+
+    @pl.loop(0, 6)
+    def _(n):
+        at = pl.ds(pl.multiple_of(n * 256, 256), 256)
+        prod = lax.dot_general(
+            hidden[...], w2n[at, :], (((1,), (1,)), ((), ())), preferred_element_type=jnp.float32
+        ).astype(jnp.bfloat16)
+        part[:, :, at] = prod.reshape(4, 128, 256)
+        fluxp[...] += jnp.dot(prod, proj[at, :], preferred_element_type=jnp.float32)
+
+    for q in range(4):
+        fluxin[q] = fluxp[128 * q : 128 * q + 128, :].astype(jnp.bfloat16)
+    kf = {}
+    for i in (2, 1, 3):
+        kf[i] = comm.send(fluxin.at[(p + i) % 4], fluxin.at[3 + i], peer(dy=2 * i))
+    mine = pl.ds(pl.multiple_of(p * 128, 128), 128)
+    total = jnp.dot(state[mine, :], proj[...], preferred_element_type=jnp.float32) + fluxp[mine, :]
+    for i in (1, 3, 2):
+        comm.recv(kf[i], fluxin.at[3 + i])
+        total = total + fluxin[3 + i].astype(jnp.float32)
+    flux_all[p] = total.astype(jnp.bfloat16)
+    kg = {}
+    for i in (2, 1, 3):
+        kg[i] = comm.send(flux_all.at[p], flux_all.at[p], peer(dy=2 * i))
+    ka = {}
+    for i in (2, 1, 3):
+        ka[i] = comm.send(part.at[(p + i) % 4], partin.at[i - 1], peer(dy=2 * i))
+    for i in (1, 3, 2):
+        comm.recv(kg[i], flux_all.at[(p - i + 4) % 4])
+    for i in (1, 3, 2):
+        comm.recv(ka[i], partin.at[i - 1])
+
+    @pl.loop(0, 8)
+    def _(n):
+        at = pl.ds(pl.multiple_of(n * 16, 16), 16)
+        acc = part[p, at, :].astype(jnp.float32)
+        for i in range(3):
+            acc = acc + partin[i, at, :].astype(jnp.float32)
+        own_rows = state[pl.ds(pl.multiple_of(p * 128 + n * 16, 16), 16), :].astype(jnp.float32)
+        atmos_out[at, :] = (own_rows + acc).astype(jnp.bfloat16)
+
+    comm.drain()
+
+
+def vmem(shape, dtype):
+    return pltpu.VMEM(shape, dtype)
+
+
+WHOLE = pl.BlockSpec(memory_space=pltpu.VMEM)
+
+
+def atmos_call(state, gain, w1, w2, proj):
+    bf = jnp.bfloat16
+    f32 = jnp.float32
+    copies = 256
+    return pl.pallas_call(
+        atmos_kernel,
+        out_shape=(jax.ShapeDtypeStruct((128, 1536), bf), jax.ShapeDtypeStruct((4, 128, 256), bf)),
+        in_specs=[WHOLE] * 5,
+        out_specs=(WHOLE, WHOLE),
+        scratch_shapes=[
+            vmem((4, 2, 16, 768), bf),
+            vmem((2, 48, 768), f32),
+            vmem((4, 8, 48, 768), bf),
+            vmem((4, 8, 48, 768), bf),
+            vmem((1536, 768), bf),
+            vmem((1536, 768), bf),
+            vmem((512, 1536), bf),
+            vmem((512, 768), bf),
+            vmem((4, 128, 1536), bf),
+            vmem((512, 256), f32),
+            vmem((7, 128, 256), bf),
+            vmem((3, 128, 1536), bf),
+            pltpu.SemaphoreType.DMA((copies,)),
+            pltpu.SemaphoreType.DMA((copies,)),
+        ],
+        compiler_params=pltpu.CompilerParams(
+            collective_id=0, has_side_effects=True, vmem_limit_bytes=48 << 20
+        ),
+        name="atmos",
+    )(state, gain, w1, w2, proj)
+
+
+def grads_peers():
+    out = [peer(dc=1)]
+    out += [peer(dx=i) for i in (1, 2, 3)]
+    out += [peer(dz=i) for i in range(1, 8)]
+    out += [peer(dy=i) for i in range(1, 8)]
+    return out
+
+
+def grads_kernel(
+    terms, out, out16, core_in, sum0, part_x, part_z, x_in, z_in, part_xz, part_zx, xz_in, zx_in,
+    part_y, y_in, send_sems, recv_sems,
+):
+    x, y, z, c = coords()
+    comm = Comm(send_sems, recv_sems)
+    f32 = jnp.float32
+    bf = jnp.bfloat16
+    for b in range(2):
+
+        @pl.loop(0, 64)
+        def _(n):
+            out16[b, n] = terms[n, b].astype(bf)
+
+    barrier(grads_peers())
+    k = comm.send(out16.at[1 - c], core_in, peer(dc=1))
+    comm.recv(k, core_in)
+
+    @pl.loop(0, 32)
+    def _(n):
+        part_x[n // 8, n % 8] = (terms[n, c] + core_in[n].astype(f32)).astype(bf)
+        m = n + 32
+        part_z[n % 8, n // 8] = (terms[m, c] + core_in[m].astype(f32)).astype(bf)
+
+    kx = {}
+    kz = {}
+    for i in (4, 3, 5, 2, 6, 1, 7):
+        kz[i] = comm.send(part_z.at[(z + i) % 8], z_in.at[i - 1], peer(dz=i))
+        if i in (1, 2, 3):
+            kx[i] = comm.send(part_x.at[(x + i) % 4], x_in.at[i - 1], peer(dx=i))
+    for i in (1, 3, 2):
+        comm.recv(kx[i], x_in.at[i - 1])
+    for n in range(8):
+        acc = terms[x * 8 + n, c] + core_in[x * 8 + n].astype(f32)
+        for i in range(3):
+            acc = acc + x_in[i, n].astype(f32)
+        sum0[n] = acc
+        part_xz[n] = acc.astype(bf)
+    kxz = {}
+    for i in (4, 3, 5, 2, 6, 1, 7):
+        kxz[i] = comm.send(part_xz.at[(z + i) % 8], xz_in.at[i - 1], peer(dz=i))
+    for i in (1, 7, 2, 6, 3, 5, 4):
+        comm.recv(kz[i], z_in.at[i - 1])
+    for n in range(4):
+        m = 32 + n * 8 + z
+        acc = terms[m, c] + core_in[m].astype(f32)
+        for i in range(7):
+            acc = acc + z_in[i, n].astype(f32)
+        sum0[8 + n] = acc
+        part_zx[n] = acc.astype(bf)
+    kzx = {}
+    for i in (2, 1, 3):
+        kzx[i] = comm.send(part_zx.at[(x + i) % 4], zx_in.at[i - 1], peer(dx=i))
+    for i in (1, 7, 2, 6, 3, 5, 4):
+        comm.recv(kxz[i], xz_in.at[i - 1])
+    acc = sum0[z]
+    for i in range(7):
+        acc = acc + xz_in[i].astype(f32)
+    for q in range(4):
+        part_y[2 * q, 0:4, :] = acc[4 * q : 4 * q + 4, :]
+        part_y[2 * q, 4:8, :] = jnp.zeros((4, 256), f32)
+    for i in (1, 3, 2):
+        comm.recv(kzx[i], zx_in.at[i - 1])
+    acc = sum0[8 + x]
+    for i in range(3):
+        acc = acc + zx_in[i].astype(f32)
+    for q in range(4):
+        part_y[2 * q + 1, 0:4, :] = acc[4 * q : 4 * q + 4, :]
+        part_y[2 * q + 1, 4:8, :] = jnp.zeros((4, 256), f32)
+    ky = {}
+    for i in (4, 3, 5, 2, 6, 1, 7):
+        ky[i] = comm.send(part_y.at[(y + i) % 8], y_in.at[i - 1], peer(dy=i))
+    acc = part_y[y]
+    for i in (1, 7, 2, 6, 3, 5, 4):
+        comm.recv(ky[i], y_in.at[i - 1])
+        acc = acc + y_in[i - 1]
+    out[...] = acc[0:4, :]
+    comm.drain()
+
+
+def grads_call(terms):
+    bf = jnp.bfloat16
+    f32 = jnp.float32
+    copies = 64
+    return pl.pallas_call(
+        grads_kernel,
+        out_shape=jax.ShapeDtypeStruct((4, 256), f32),
+        in_specs=[WHOLE],
+        out_specs=WHOLE,
+        scratch_shapes=[
+            vmem((2, 64, 16, 256), bf),
+            vmem((64, 16, 256), bf),
+            vmem((12, 16, 256), f32),
+            vmem((4, 8, 16, 256), bf),
+            vmem((8, 4, 16, 256), bf),
+            vmem((3, 8, 16, 256), bf),
+            vmem((7, 4, 16, 256), bf),
+            vmem((8, 16, 256), bf),
+            vmem((4, 16, 256), bf),
+            vmem((7, 16, 256), bf),
+            vmem((3, 16, 256), bf),
+            vmem((8, 8, 256), f32),
+            vmem((7, 8, 256), f32),
+            pltpu.SemaphoreType.DMA((copies,)),
+            pltpu.SemaphoreType.DMA((copies,)),
+        ],
+        compiler_params=pltpu.CompilerParams(
+            collective_id=1, has_side_effects=True, vmem_limit_bytes=32 << 20
+        ),
+        name="grads",
+    )(terms.reshape(64, 2, 16, 256))
 
 
 def with_halo(block, sides, width):
@@ -20,12 +474,6 @@
         high = lax.ppermute(lax.slice_in_dim(block, 0, width, axis=dim), axis, backward)
         block = jnp.concatenate([low, block, high], axis=dim)
     return block
-
-
-def rms_norm(values, gain):
-    wide = values.astype(jnp.float32)
-    scale = lax.rsqrt(jnp.mean(wide * wide, axis=-1, keepdims=True) + epsilon)
-    return (wide * scale * gain).astype(jnp.bfloat16)
 
 
 def on_device(
@@ -44,32 +492,11 @@
     ocean_w_out,
     ocean_cotangent,
 ):
-    normed = rms_norm(atmos_state, atmos_gain)
-    rows_all = atmos_state.shape[0]
-    hsum = jnp.dot(
-        normed,
-        lax.all_gather(w_first, ("grp", "tile"), axis=0, tiled=True),
-        preferred_element_type=jnp.float32,
-    )
-    hidden = jax.nn.gelu(hsum).astype(jnp.bfloat16)
-    partial_sum = lax.dot_general(
-        hidden,
-        lax.all_gather(w_second, ("grp", "tile"), axis=0, tiled=True),
-        (((1,), (1,)), ((), ())),
-        preferred_element_type=jnp.float32,
-    )
-    rows_own = rows_all // lax.axis_size("tp")
-    block_rows = remap_weight.shape[2]
+    atmos_out, blocks = atmos_call(
+        atmos_state, atmos_gain.reshape(1, -1), w_first, w_second, flux_proj
+    )
     channels = flux_proj.shape[1]
-    summed = lax.psum_scatter(
-        partial_sum.astype(jnp.bfloat16), "tp", scatter_dimension=0, tiled=True
-    ).astype(jnp.float32)
-    own_rows = lax.dynamic_slice_in_dim(atmos_state, lax.axis_index("tp") * rows_own, rows_own, 0)
-    atmos_out = (own_rows.astype(jnp.float32) + summed).astype(jnp.bfloat16)
-    flux = jnp.dot(atmos_out, flux_proj, preferred_element_type=jnp.float32).astype(jnp.bfloat16)
-    piece = lax.all_gather(flux, "tp", axis=0, tiled=True)
-    count = piece.shape[0] // block_rows
-    blocks = piece.reshape(count, block_rows, channels)
+    count = blocks.shape[0]
     targets = jnp.arange(count, dtype=jnp.int32)
     select = (remap_index[:, :, None] == targets[None, None, :]).astype(jnp.bfloat16)
     picked = jnp.einsum("bkj,jrc->bkrc", select, blocks, preferred_element_type=jnp.float32).astype(
@@ -123,7 +550,7 @@
         activated, dout, (((0,), (0,)), ((), ())), preferred_element_type=jnp.float32
     )
     terms = jnp.concatenate([grad_in, grad_out], axis=0)
-    weight_grads = lax.psum_scatter(terms, ("grp", "tile", "tp"), scatter_dimension=0, tiled=True)
+    weight_grads = grads_call(terms)
     return (atmos_out, ocean_out, weight_grads)
 
 

time: 842 us -> 164 us (0.19)
  waiting for transfers between devices: 768 us -> 6.9 us
  Pallas kernels: 0 us -> 133 us
  between operations: 14.1 us -> 0.91 us
  blocking collectives: 11.5 us -> 0 us
    all_gather x2 -> x0, waiting for transfers between devices: 438 us -> none  [the longest x1 223 us: on_device(): lax.all_gather(w_second, ('grp', 'tile'), axis=0, tiled=True)]
    unnamed x5 -> x0, waiting for transfers between devices: 286 us -> none
    pallas_call x0 -> x2, Pallas kernels: none -> 133 us  [the longest x1 106 us: atmos_call(): pl.pallas_call(atmos_kernel, out_shape=(jax.ShapeDtypeStruct((128, 1536),...]
    reduce_scatter x1 -> x0, waiting for transfers between devices: 43.7 us -> none  [on_device(): lax.psum_scatter(partial_sum.astype(jnp.bfloat16), 'tp', scatter_dimensio...]
    all_gather x1 -> x0, blocking collectives: 11.5 us -> none  [on_device(): piece = lax.all_gather(flux, 'tp', axis=0, tiled=True)]
  transfers between devices with their start and end apart: 8 -> 4, of which waited for: 6 -> 2; matrix products, arithmetic and copies ran while one was open for 1% -> 0% of each run, Pallas kernels for 0% -> 0%
where the time goes in v1:
time: 164 us; the launch traced here: 163 us
  Pallas kernels  133 us (81%)
  starting transfers between devices  10 us (6%)
  waiting for transfers between devices  6.9 us (4%)
  local copies, waits for them, and re-layouts  6.34 us (4%)
  matrix products  4.69 us (3%)
    pallas_call x1, Pallas kernels, atmos_call(): pl.pallas_call(atmos_kernel, out_shape=(jax.ShapeDtypeStruct((128, 1536),...  106 us
    pallas_call x1, Pallas kernels, grads_call(): pl.pallas_call(grads_kernel, out_shape=jax.ShapeDtypeStruct((4, 256), f32...  27.2 us
    ppermute x2, waiting for transfers between devices, with_halo(): lax.ppermute(lax.slice_in_dim(block, 0, width, axis=dim), axis, backward)  6.89 us
    ppermute x2, starting transfers between devices, with_halo(): lax.ppermute(lax.slice_in_dim(block, block.shape[dim] - width, None, axis...  6.82 us
    unnamed x30, local copies, waits for them, and re-layouts  5.49 us
  transfers between devices with their start and end apart: 4, of which 2 were waited for; matrix products, arithmetic and copies ran while one was open for 0% of the time, Pallas kernels for 0%

profile of v1, /device:TPU:1, one launch (start us, length us, event | category | flops | bytes accessed | tf_op | source)
XLA Modules:
  0.0 162.6 jit_solution(10246623195334638264)
XLA Ops:
  0.6 0.0 copy-start
  0.6 0.0 copy-start.12
  0.7 0.0 copy-start.10
  0.7 0.8 reshape.57.gain
  1.4 0.0 copy-start.1
  1.4 1.4 copy-done.1
  2.8 0.0 copy-start.2
  2.8 1.1 copy-done.2
  4.0 0.0 copy-start.3
  4.0 0.7 copy-done.3
  4.7 0.0 copy-start.4
  4.7 0.7 copy-done.4
  5.5 0.0 copy-start.7
  5.5 0.0 copy-start.9
  5.5 0.0 copy-start.8
  5.5 0.0 copy-start.11
  5.5 105.5 %atmos.1 = (bf16[128,1536]{1,0:T(8,128)(2,1)S(1)}, bf16[4,128,256]{2,1,0:T(8,128)(2,1)S(1)}) custom-call(bf16[512,1536]{1,0:T(8,128)(2,1)S(1)} %copy-done.1, f32[1,1536]{1,0:T(1,128)S(1)} %reshape.57.gain, bf16[12,768]{1,0:T(8,128)(2,1)S(1)} %copy-done.3, bf16[12,768]{1,0:T(8,128)(2,1)S(1)} %copy-done.4, bf16[1536,256]{1,0:T(8,128)(2,1)S(1)} %copy-done.2), custom_call_target="tpu_custom_call" | custom-call | tf_op jit(solution)/shard_map/atmos/pallas_call | solution.py:317
  111.0 0.0 copy-done.12
  111.0 0.4 fusion.22
  111.4 0.0 copy-done.7
  111.4 0.2 fusion.2
  111.6 0.0 copy-done.10
  111.6 0.0 copy-done.9
  111.6 0.1 select_convert_fusion
  111.8 0.0 copy-start.13
  111.8 3.9 %collective-permute-start = (bf16[1,32,256]{2,1,0:T(8,128)(2,1)S(1)}, bf16[1,32,256]{2,1,0:T(8,128)(2,1)S(1)}, u32[]{:S(2)}, u32[]{:S(2)}) collective-permute-start(bf16[1,32,256]{2,1,0:T(8,128)(2,1)S(1)} %get-tuple-element.11), channel_id=1, source_target_pairs={{0,4},{4,8},{8,12},{12,16},{16,20},{20,24},{24,28},{28,32},{32,36}... | collective-permute-start | bytes 49160 | tf_op jit(solution)/shard_map/ppermute | solution.py:471
  115.7 1.9 %collective-permute-start.1 = (bf16[1,32,256]{2,1,0:T(8,128)(2,1)S(1)}, bf16[1,32,256]{2,1,0:T(8,128)(2,1)S(1)}, u32[]{:S(2)}, u32[]{:S(2)}) collective-permute-start(bf16[1,32,256]{2,1,0:T(8,128)(2,1)S(1)} %get-tuple-element.12), channel_id=1, source_target_pairs={{4,0},{8,4},{12,8},{16,12},{20,16},{24,20},{28,24},{32,28},{36,32}... | collective-permute-start | bytes 49160 | tf_op jit(solution)/shard_map/ppermute | solution.py:474
  117.6 0.1 lt.23
  117.7 0.0 copy-done.8
  117.7 0.1 fusion.13
  117.8 0.0 copy-start.6
  117.8 0.0 collective-permute-done
  117.8 2.9 %collective-permute-done.1 = bf16[1,32,256]{2,1,0:T(8,128)(2,1)S(1)} collective-permute-done((bf16[1,32,256]{2,1,0:T(8,128)(2,1)S(1)}, bf16[1,32,256]{2,1,0:T(8,128)(2,1)S(1)}, u32[]{:S(2)}, u32[]{:S(2)}) %collective-permute-start.1) | collective-permute-done | bytes 16416 | tf_op jit(solution)/shard_map/ppermute | solution.py:474
  120.7 2.9 %collective-permute-start.2 = (bf16[10,1,256]{2,1,0:T(2,128)(2,1)S(1)}, bf16[10,1,256]{2,1,0:T(2,128)(2,1)S(1)}, u32[]{:S(2)}, u32[]{:S(2)}) collective-permute-start(bf16[10,1,256]{2,1,0:T(2,128)(2,1)S(1)} %get-tuple-element.9), channel_id=1, source_target_pairs={{0,1},{1,2},{2,3},{4,5},{5,6},{6,7},{8,9},{9,10},{10,11},{12,13},{... | collective-permute-start | bytes 15368 | tf_op jit(solution)/shard_map/ppermute | solution.py:471
  123.7 1.3 collective-permute-start.3
  125.0 0.0 copy-done.11
  125.0 0.0 collective-permute-done.2
  125.0 4.0 %collective-permute-done.3 = bf16[10,1,256]{2,1,0:T(2,128)(2,1)S(1)} collective-permute-done((bf16[10,1,256]{2,1,0:T(2,128)(2,1)S(1)}, bf16[10,1,256]{2,1,0:T(2,128)(2,1)S(1)}, u32[]{:S(2)}, u32[]{:S(2)}) %collective-permute-start.3) | collective-permute-done | bytes 5152 | tf_op jit(solution)/shard_map/ppermute | solution.py:474
  129.0 0.1 maximum_convert_fusion
  129.1 0.3 fusion.34
  129.4 0.2 multiply_reduce_fusion
  129.6 0.0 copy-done.13
  129.6 0.1 multiply_convert_fusion.1
  129.7 0.0 copy-done.6
  129.7 0.3 fusion.40
  130.0 0.6 fusion.33
  130.6 0.0 copy-done
  130.6 2.1 %fusion.11 = f32[1024,256]{1,0:T(8,128)} fusion(bf16[256,256]{1,0:T(8,128)(2,1)S(1)} %bitcast.46, f32[256,1024]{1,0:T(8,128)S(1)} %fusion.40, bf16[256,256]{1,0:T(8,128)(2,1)S(1)} %fusion.13, bf16[1024,256]{1,0:T(8,128)(2,1)S(1)} %copy-done), kind=kOutput, calls=%fused_computation.18 | convolution fusion | flops 273678336 | bytes 2883584 | tf_op jit(solution)/shard_map/dot_general | solution.py:546
  132.7 0.0 copy-start.5
  132.7 1.1 fusion.3
  133.9 0.1 copy-done.5
  134.0 0.1 pad_maximum_fusion
  134.1 27.2 %grads.1 = f32[4,256]{1,0:T(4,128)S(1)} custom-call(f32[64,2,16,256]{3,2,1,0:T(8,128)S(1)} %bitcast.41), custom_call_target="tpu_custom_call" | custom-call | tf_op jit(solution)/shard_map/grads/pallas_call | solution.py:437
  161.3 0.7 copy.27
  162.0 0.6 copy.28
  (6 shorter events, 0.1 us)
Async XLA Ops:
  0.6 130.0 %copy-start = (bf16[1024,256]{1,0:T(8,128)(2,1)S(1)}, bf16[1024,256]{1,0:T(8,128)(2,1)}, u32[]{:S(2)}) copy-start(bf16[1024,256]{1,0:T(8,128)(2,1)} %param.26) | copy-start | bytes 1572868
  0.6 110.4 %copy-start.12 = (s32[2,3]{1,0:T(2,128)S(1)}, s32[2,3]{1,0:T(2,128)}, u32[]{:S(2)}) copy-start(s32[2,3]{1,0:T(2,128)} %param.19) | copy-start | bytes 76
  0.7 111.0 %copy-start.10 = (s32[8,32]{1,0:T(8,128)S(1)}, s32[8,32]{1,0:T(8,128)}, u32[]{:S(2)}) copy-start(s32[8,32]{1,0:T(8,128)} %param.22) | copy-start | bytes 3076
  1.4 1.4 copy-start.1
  2.8 1.1 copy-start.2
  4.0 0.7 copy-start.3
  4.7 0.7 copy-start.4
  5.5 105.9 %copy-start.7 = (bf16[2,3,128,128]{3,2,1,0:T(8,128)(2,1)S(1)}, bf16[2,3,128,128]{3,2,1,0:T(8,128)(2,1)}, u32[]{:S(2)}) copy-start(bf16[2,3,128,128]{3,2,1,0:T(8,128)(2,1)} %param.20) | copy-start | bytes 589828
  5.5 106.2 %copy-start.9 = (bf16[8,32,256]{2,1,0:T(8,128)(2,1)S(1)}, bf16[8,32,256]{2,1,0:T(8,128)(2,1)}, u32[]{:S(2)}) copy-start(bf16[8,32,256]{2,1,0:T(8,128)(2,1)} %param.21) | copy-start | bytes 393220
  5.5 112.2 %copy-start.8 = (bf16[8,32,256]{2,1,0:T(8,128)(2,1)S(1)}, bf16[8,32,256]{2,1,0:T(8,128)(2,1)}, u32[]{:S(2)}) copy-start(bf16[8,32,256]{2,1,0:T(8,128)(2,1)} %param.27) | copy-start | bytes 393220
  5.5 119.5 %copy-start.11 = (f32[3,3,256]{2,1,0:T(4,128)S(1)}, f32[3,3,256]{2,1,0:T(4,128)}, u32[]{:S(2)}) copy-start(f32[3,3,256]{2,1,0:T(4,128)} %param.23) | copy-start | bytes 27652
  111.8 17.8 %copy-start.13 = (f32[256]{0:T(256)S(1)}, f32[256]{0:T(256)}, u32[]{:S(2)}) copy-start(f32[256]{0:T(256)} %param.24) | copy-start | bytes 3076
  111.8 6.0 %collective-permute-start = (bf16[1,32,256]{2,1,0:T(8,128)(2,1)S(1)}, bf16[1,32,256]{2,1,0:T(8,128)(2,1)S(1)}, u32[]{:S(2)}, u32[]{:S(2)}) collective-permute-start(bf16[1,32,256]{2,1,0:T(8,128)(2,1)S(1)} %get-tuple-element.11), channel_id=1, source_target_pairs={{0,4},{4,8},{8,12},{12,16},{16,20},{20,24},{24,28},{28,32},{32,36}... | collective-permute-start | bytes 49160 | tf_op jit(solution)/shard_map/ppermute | solution.py:471
  115.7 5.1 %collective-permute-start.1 = (bf16[1,32,256]{2,1,0:T(8,128)(2,1)S(1)}, bf16[1,32,256]{2,1,0:T(8,128)(2,1)S(1)}, u32[]{:S(2)}, u32[]{:S(2)}) collective-permute-start(bf16[1,32,256]{2,1,0:T(8,128)(2,1)S(1)} %get-tuple-element.12), channel_id=1, source_target_pairs={{4,0},{8,4},{12,8},{16,12},{20,16},{24,20},{28,24},{32,28},{36,32}... | collective-permute-start | bytes 49160 | tf_op jit(solution)/shard_map/ppermute | solution.py:474
  117.8 11.9 %copy-start.6 = (bf16[256,1024]{1,0:T(8,128)(2,1)S(1)}, bf16[256,1024]{1,0:T(8,128)(2,1)}, u32[]{:S(2)}) copy-start(bf16[256,1024]{1,0:T(8,128)(2,1)} %param.25) | copy-start | bytes 1572868
  120.7 4.3 %collective-permute-start.2 = (bf16[10,1,256]{2,1,0:T(2,128)(2,1)S(1)}, bf16[10,1,256]{2,1,0:T(2,128)(2,1)S(1)}, u32[]{:S(2)}, u32[]{:S(2)}) collective-permute-start(bf16[10,1,256]{2,1,0:T(2,128)(2,1)S(1)} %get-tuple-element.9), channel_id=1, source_target_pairs={{0,1},{1,2},{2,3},{4,5},{5,6},{6,7},{8,9},{9,10},{10,11},{12,13},{... | collective-permute-start | bytes 15368 | tf_op jit(solution)/shard_map/ppermute | solution.py:471
  123.7 5.3 %collective-permute-start.3 = (bf16[10,1,256]{2,1,0:T(2,128)(2,1)S(1)}, bf16[10,1,256]{2,1,0:T(2,128)(2,1)S(1)}, u32[]{:S(2)}, u32[]{:S(2)}) collective-permute-start(bf16[10,1,256]{2,1,0:T(2,128)(2,1)S(1)} %get-tuple-element.10), channel_id=1, source_target_pairs={{1,0},{2,1},{3,2},{5,4},{6,5},{7,6},{9,8},{10,9},{11,10},{13,12},{... | collective-permute-start | bytes 15368 | tf_op jit(solution)/shard_map/ppermute | solution.py:474
  132.7 1.2 copy-start.5

commit v2 on v1

v2 whole, which is shorter than its diff:
```python
import jax
import jax.numpy as jnp
from jax import lax
from jax.experimental import pallas as pl
from jax.experimental.pallas import tpu as pltpu
from jax.sharding import PartitionSpec as P

LEV = 16
MESH = pl.DeviceIdType.MESH
epsilon = 1e-06


def coords():
    g = lax.axis_index("grp")
    t = lax.axis_index("tile")
    p = lax.axis_index("tp")
    return t // 16, p * 2 + g, (t // 2) % 8, t % 2


def device_at(x, y, z, c):
    return (y % 2, x * 16 + z * 2 + c, y // 2)


def peer(dx=0, dy=0, dz=0, dc=0):
    x, y, z, c = coords()
    return device_at((x + dx) % 4, (y + dy) % 8, (z + dz) % 8, (c + dc) % 2)


class Comm:
    def __init__(self, send_sems, recv_sems):
        self.send_sems = send_sems
        self.recv_sems = recv_sems
        self.count = 0
        self.sent = []

    def send(self, src, dst, dev):
        k = self.count
        self.count += 1
        copy = pltpu.make_async_remote_copy(
            src_ref=src,
            dst_ref=dst,
            send_sem=self.send_sems.at[k],
            recv_sem=self.recv_sems.at[k],
            device_id=dev,
            device_id_type=MESH,
        )
        copy.start()
        self.sent.append(copy)
        return k

    def recv(self, k, ref):
        pltpu.make_async_remote_copy(
            src_ref=ref,
            dst_ref=ref,
            send_sem=self.send_sems.at[k],
            recv_sem=self.recv_sems.at[k],
            device_id=peer(dc=1),
            device_id_type=MESH,
        ).wait_recv()

    def drain(self):
        for copy in self.sent:
            copy.wait_send()
        self.sent = []


def gelu(v):
    return 0.5 * v * (1.0 + jnp.tanh(0.7978845608028654 * (v + 0.044715 * (v * v * v))))


def near(df, dp):
    f = lax.axis_index("grp") * 64 + lax.axis_index("tile")
    f = (f + df + 128) % 128
    return (f // 64, f % 64, (lax.axis_index("tp") + dp + 4) % 4)


def all_peers():
    x, y, z, c = coords()
    y_pair = y + 1 - 2 * (y % 2)
    out = [peer(dc=1), device_at(x, y_pair, z, 1 - c)]
    out += [peer(dx=i) for i in (1, 2, 3)]
    out += [peer(dz=i) for i in range(1, 8)]
    out += [peer(dy=i) for i in range(1, 8)]
    out += [near(df, dp) for df in (1, -1) for dp in (0, 1, -1)]
    return out


def kernel(
    w1_hbm, w2_hbm, state_hbm, proj_hbm, remap_hbm, ocean_hbm, cot_hbm, win_hbm, wout_hbm,
    gain, depth, taps, ocean_gain, pick,
    atmos_out, ocean_out, grads_out,
    w1, w2, state, proj, remap, ocean, cot, win, wout,
    stage, compose, g1, g2, w1n, w2n, normed, hidden, part, proj_t, wf_t, fluxp, fluxin, flux_all,
    relay_in, relay_sum, direct_in, summed_in,
    wet, dout, dact, fpad, edge, edge_in, corner_in, onorm, oacc,
    terms, out16, core_in, sum0, part_x, part_z, x_in, z_in, part_xz, part_zx, xz_in, zx_in,
    part_y, y_in,
    local_sems, send_sems, recv_sems,
):
    bf = jnp.bfloat16
    f32 = jnp.float32
    x, y, z, c = coords()
    g = y % 2
    p = y // 2
    y_pair = y + 1 - 2 * g
    comm = Comm(send_sems, recv_sems)
    peers = all_peers()
    entry = pltpu.get_barrier_semaphore()
    for dev in peers:
        pl.semaphore_signal(entry, inc=1, device_id=dev, device_id_type=MESH)
    pairs = (
        (w1_hbm, w1), (w2_hbm, w2), (proj_hbm, proj), (state_hbm, state), (remap_hbm, remap),
        (ocean_hbm, ocean), (cot_hbm, cot), (win_hbm, win), (wout_hbm, wout),
    )
    loads = [
        pltpu.make_async_copy(src, dst, local_sems.at[n]) for n, (src, dst) in enumerate(pairs)
    ]
    for load in loads:
        load.start()
    slot = 2 * g + c
    stage[slot] = jnp.zeros(stage.shape[1:], stage.dtype)
    loads[0].wait()
    loads[1].wait()
    stage[slot, 0, 0:12, :] = w1[...]
    stage[slot, 1, 0:12, :] = w2[...]
    loads[2].wait()
    for n in range(6):
        at = slice(256 * n, 256 * n + 256)
        proj_t[:, at] = proj[at, :].astype(f32).T.astype(bf)
    pl.semaphore_wait(entry, len(peers))

    own = stage.at[slot]
    k_core = comm.send(own, own, device_at(x, y, z, 1 - c))
    k_pair = comm.send(own, own, device_at(x, y_pair, z, c))
    k_diag = comm.send(own, own, device_at(x, y_pair, z, 1 - c))
    loads[3].wait()
    rows = 64

    @pl.loop(0, state.shape[0] // rows)
    def _(i):
        at = pl.ds(pl.multiple_of(i * rows, rows), rows)
        wide = state[at, :].astype(f32)
        scale = lax.rsqrt(jnp.mean(wide * wide, axis=-1, keepdims=True) + epsilon)
        normed[at, :] = (wide * scale * gain[...]).astype(bf)

    half = pl.ds(pl.multiple_of(c * 384, 128), 384)
    other = pl.ds(pl.multiple_of((1 - c) * 384, 128), 384)
    comm.recv(k_core, stage.at[2 * g + 1 - c])
    comm.recv(k_pair, stage.at[2 * (1 - g) + c])
    comm.recv(k_diag, stage.at[2 * (1 - g) + 1 - c])
    for w, dest in ((0, g1), (1, g2)):
        for s in range(4):
            compose[w, 12 * s : 12 * s + 12, :] = stage[s, w, :, half].astype(f32)[0:12, :]
        dest[x, z, :, half] = compose[w].astype(bf)

    def xi(i):
        return (x + i + 4) % 4

    def zi(i):
        return (z + i + 8) % 8

    handed = []
    every = pl.ds(0, 48)
    low = pl.ds(0, 32)
    high = pl.ds(32, 16)

    def send1(i, at, dev):
        ref = g1.at[xi(i), at, every, half]
        return comm.send(ref, ref, dev)

    def send2(at, j, dev, piece=every):
        ref = g2.at[at, zi(j), piece, half]
        return comm.send(ref, ref, dev)

    def hand1(at):
        ref = g1.at[:, at, :, half]
        handed.append((comm.send(ref, ref, peer(dc=1)), g1.at[:, at, :, other]))

    def hand2(at):
        ref = g2.at[at, :, :, half]
        handed.append((comm.send(ref, ref, peer(dc=1)), g2.at[at, :, :, other]))

    k2z = {}
    k1x = {}
    k1z = {}
    k2x = {}
    for d in (1, -1):
        k2z[1, d] = send2(x, 0, peer(dz=d))
    for i in (1, 3, 2):
        k1x[i] = send1(0, z, peer(dx=i))
    for d in (1, -1):
        k2z[2, d] = send2(x, 0, peer(dz=2 * d))

    def start_2x(j):
        for d in (1, -1):
            k2x[1, j, d] = send2(x, j, peer(dx=d))

    def start_1z(i):
        for d in (1, -1):
            k1z[1, i, d] = send1(i, z, peer(dz=d))

    start_2x(0)
    start_1z(0)
    for d in (1, -1):
        comm.recv(k2z[1, d], g2.at[x, zi(-d), every, half])
        start_2x(-d)
    for i in (1, 3):
        comm.recv(k1x[i], g1.at[xi(-i), z, every, half])
    for d in (1, -1):
        comm.recv(k2z[2, d], g2.at[x, zi(-2 * d), every, half])
        k2z[3, d] = send2(x, -2 * d, peer(dz=d))
        k2z[4, d] = send2(x, -2 * d, peer(dz=2 * d), low if d == 1 else high)
        start_2x(-2 * d)
    for i in (1, 3):
        start_1z(-i % 4)
    comm.recv(k1x[2], g1.at[xi(2), z, every, half])
    start_1z(2)
    hand1(z)

    order_1 = (0, 3, 1, 2)

    def round_1z(r, n):
        i = order_1[n]
        for d in (1, -1):
            at = zi(-r * d)
            if r == 4 and (n < 2) != (d == 1):
                continue
            comm.recv(k1z[r, i, d], g1.at[xi(i), at, every, half])
            if r < 3 or (r == 3 and (n < 2) == (d == 1)):
                k1z[r + 1, i, d] = send1(i, at, peer(dz=d))
            if n == 3 and r < 4:
                hand1(at)
        if n == 3 and r == 4:
            hand1(zi(4))

    order_2 = (0, -1, 1, -2, 2, -3, 3, 4)

    def round_2x(r, n):
        j = order_2[n]
        for d in (1, -1):
            at = xi(-r * d)
            if r == 2 and (n < 4) != (d == 1):
                continue
            comm.recv(k2x[r, j, d], g2.at[at, zi(j), every, half])
            if r == 1 and (n < 4) == (d == 1):
                k2x[2, j, d] = send2(at, j, peer(dx=d))
            if n == 7 and r == 1:
                hand2(at)
        if n == 7 and r == 2:
            hand2(xi(2))

    round_2x(1, 0)
    round_1z(1, 0)
    round_2x(1, 1)
    for d in (1, -1):
        comm.recv(k2z[3, d], g2.at[x, zi(-3 * d), every, half])
        start_2x(-3 * d)
    for d in (1, -1):
        comm.recv(k2z[4, d], g2.at[x, zi(4), low if d == 1 else high, half])
    start_2x(4)
    hand2(x)
    round_1z(1, 1)
    round_2x(1, 2)
    round_1z(1, 2)
    round_2x(1, 3)
    round_1z(1, 3)
    later_2x = [(1, n) for n in range(4, 8)] + [(2, n) for n in range(8)]
    later_1z = [(2, n) for n in range(4)] + [(3, n) for n in range(4)] + [(4, n) for n in range(4)]
    while later_1z or later_2x:
        if later_1z:
            round_1z(*later_1z.pop(0))
        if later_2x:
            round_2x(*later_2x.pop(0))

    for k, ref in handed:
        comm.recv(k, ref)

    def in_order(src, dst):
        @pl.loop(0, 16)
        def _(j):
            a = src[j // 4, 2 * (j % 4)].astype(f32)
            b = src[j // 4, 2 * (j % 4) + 1].astype(f32)
            at = pl.multiple_of(j * 48, 16)
            dst[pl.ds(at, 48), :] = jnp.concatenate([a[:24], b[:24]], axis=0).astype(bf)
            dst[pl.ds(768 + at, 48), :] = jnp.concatenate([a[24:], b[24:]], axis=0).astype(bf)

    in_order(g1, w1n)
    in_order(g2, w2n)

    @pl.loop(0, 3)
    def _(n):
        at = pl.ds(pl.multiple_of(n * 256, 256), 256)
        pre = jnp.dot(normed[...], w1n[:, at], preferred_element_type=f32)
        hidden[:, at] = gelu(pre).astype(bf)
        wf_t[:, at] = jnp.dot(proj_t[...], w2n[:, at], preferred_element_type=f32).astype(bf)

    for q in range(4):
        fp = lax.dot_general(
            hidden[128 * q : 128 * q + 128, :], wf_t[...], (((1,), (1,)), ((), ())),
            preferred_element_type=f32,
        )
        fluxp[q] = fp
        fluxin[q] = fp.astype(bf)
    kf = {}
    for i in (2, 1, 3):
        kf[i] = comm.send(fluxin.at[(p + i) % 4], fluxin.at[3 + i], peer(dy=2 * i))
    mine = pl.ds(pl.multiple_of(p * 128, 128), 128)
    total = jnp.dot(state[mine, :], proj[...], preferred_element_type=f32) + fluxp[p]

    @pl.loop(0, 6)
    def _(n):
        at = pl.ds(pl.multiple_of(n * 256, 256), 256)
        prod = lax.dot_general(
            hidden[...], w2n[at, :], (((1,), (1,)), ((), ())), preferred_element_type=f32
        ).astype(bf)
        part[:, :, at] = prod.reshape(4, 128, 256)

    for i in (1, 3, 2):
        comm.recv(kf[i], fluxin.at[3 + i])
        total = total + fluxin[3 + i].astype(f32)
    flux_all[p] = total.astype(bf)
    kg = {}
    for i in (2, 1, 3):
        kg[i] = comm.send(flux_all.at[p], flux_all.at[p], peer(dy=2 * i))

    for load in loads[4:]:
        load.wait()
    level = (lax.broadcasted_iota(jnp.int32, (32, 256), 1) // 16).astype(f32)
    diagonal = lax.broadcasted_iota(jnp.int32, (32, 32), 0) == lax.broadcasted_iota(
        jnp.int32, (32, 32), 1
    )
    for r in range(8):
        row = jnp.broadcast_to(depth[r : r + 1, :].astype(f32), (32, 32))
        deep = jnp.sum(jnp.where(diagonal, row, 0.0), axis=1, keepdims=True)
        is_wet = jnp.where(level < deep, 1.0, 0.0)
        at = slice(32 * r, 32 * r + 32)
        wet[at, :] = is_wet
        dout[at, :] = (cot[r].astype(f32) * is_wet).astype(bf)
    for n in range(4):
        at = slice(256 * n, 256 * n + 256)
        dact[:, at] = lax.dot_general(
            dout[...], wout[at, :], (((1,), (1,)), ((), ())), preferred_element_type=f32
        )
    for i in (1, 3, 2):
        comm.recv(kg[i], flux_all.at[(p - i + 4) % 4])

    for b in range(2):
        acc = jnp.zeros((128, 256), f32)
        for k in range(3):
            acc = acc + jnp.dot(remap[b, k], flux_all[pick[b, k]], preferred_element_type=f32)
        moved = acc.astype(bf).astype(f32)
        base = ocean[4 * b : 4 * b + 4].astype(f32).reshape(128, 256)
        field = ((base + moved) * wet[128 * b : 128 * b + 128, :]).astype(bf).astype(f32)
        fpad[1 + 4 * b : 5 + 4 * b, 8:40, :] = field.reshape(4, 32, 256)
    inner = pl.ds(8, 32)
    k_down = comm.send(fpad.at[1, inner], fpad.at[9, inner], near(-1, 0))
    k_up = comm.send(fpad.at[8, inner], fpad.at[0, inner], near(1, 0))
    for r in range(8):
        edge[0, r : r + 1, :] = fpad[1 + r, 8:9, :]
        edge[1, r : r + 1, :] = fpad[1 + r, 39:40, :]
    ke = [
        comm.send(edge.at[0], edge_in.at[0], near(0, -1)),
        comm.send(edge.at[1], edge_in.at[1], near(0, 1)),
    ]
    kc = [
        comm.send(edge.at[0], corner_in.at[0], near(1, -1)),
        comm.send(edge.at[0], corner_in.at[1], near(-1, -1)),
        comm.send(edge.at[1], corner_in.at[2], near(1, 1)),
        comm.send(edge.at[1], corner_in.at[3], near(-1, 1)),
    ]

    left_cols = pl.ds(0, 768)
    right_cols = pl.ds(768, 768)
    up = peer(dy=2)
    down = peer(dy=6)
    kr = [
        comm.send(part.at[(p + 2) % 4, :, left_cols], relay_in.at[0], down),
        comm.send(part.at[(p + 2) % 4, :, right_cols], relay_in.at[1], up),
    ]
    kd = [
        comm.send(part.at[(p + 1) % 4, :, left_cols], direct_in.at[0], up),
        comm.send(part.at[(p + 3) % 4, :, right_cols], direct_in.at[1], down),
    ]

    first = g * 64 + x * 16 + z * 2 + c
    comm.recv(k_down, fpad.at[9, inner])
    comm.recv(k_up, fpad.at[0, inner])
    for n in range(2):
        comm.recv(ke[n], edge_in.at[n])
    for n in range(4):
        comm.recv(kc[n], corner_in.at[n])
    has_left = p > 0
    has_right = p < 3
    for r in range(8):
        fpad[1 + r, 40:41, :] = jnp.where(has_right, edge_in[0, r : r + 1, :], 0.0)
        fpad[1 + r, 7:8, :] = jnp.where(has_left, edge_in[1, r : r + 1, :], 0.0)
    fpad[0, 40:41, :] = jnp.where(has_right, corner_in[0, 7:8, :], 0.0)
    fpad[9, 40:41, :] = jnp.where(has_right, corner_in[1, 0:1, :], 0.0)
    fpad[0, 7:8, :] = jnp.where(has_left, corner_in[2, 7:8, :], 0.0)
    fpad[9, 7:8, :] = jnp.where(has_left, corner_in[3, 0:1, :], 0.0)
    fpad[0] = jnp.where(first > 0, fpad[0], 0.0)
    fpad[9] = jnp.where(first < 127, fpad[9], 0.0)

    @pl.loop(0, 8)
    def _(r):
        conv = jnp.zeros((32, 256), f32)
        for i in range(3):
            for j in range(3):
                conv = conv + taps[i, j : j + 1, :] * fpad[r + i, 7 + j : 39 + j, :]
        centred = conv - jnp.mean(conv, axis=-1, keepdims=True)
        variance = jnp.mean(centred * centred, axis=-1, keepdims=True)
        at = pl.ds(pl.multiple_of(r * 32, 32), 32)
        onorm[at, :] = (centred * lax.rsqrt(variance + epsilon) * ocean_gain[...]).astype(bf)

    kcore = []
    for n in range(4):
        at = slice(256 * n, 256 * n + 256)
        pre = jnp.dot(onorm[...], win[:, at], preferred_element_type=f32)
        square = pre * pre
        tanh = jnp.tanh(0.7978845608028654 * (pre + 0.044715 * (square * pre)))
        gate = 0.5 * (1.0 + tanh)
        act = (pre * gate).astype(bf)
        slope = gate + 0.5 * pre * (1.0 - tanh * tanh) * (
            0.7978845608028654 * (1.0 + 0.134145 * square)
        )
        dpre = (slope * dact[:, at]).astype(bf)
        over_cells = (((0,), (0,)), ((), ()))
        for m, term in (
            (8 * n, lax.dot_general(dpre, onorm[...], over_cells, preferred_element_type=f32)),
            (32 + 8 * n, lax.dot_general(act, dout[...], over_cells, preferred_element_type=f32)),
        ):
            term = term.reshape(8, 2, 16, 256)
            terms[m : m + 8] = term
            out16[0, m : m + 8] = term[:, 0].astype(bf)
            out16[1, m : m + 8] = term[:, 1].astype(bf)
            to = pl.ds(m, 8)
            kcore.append((comm.send(out16.at[1 - c, to], core_in.at[to], peer(dc=1)), core_in.at[to]))
        more = jnp.dot(act, wout[at, :], preferred_element_type=f32)
        if n == 0:
            oacc[...] = more
        else:
            oacc[...] += more

    for k, ref in kcore:
        comm.recv(k, ref)

    @pl.loop(0, 32)
    def _(n):
        part_x[n // 8, n % 8] = (terms[n, c] + core_in[n].astype(f32)).astype(bf)
        m = n + 32
        part_z[n % 8, n // 8] = (terms[m, c] + core_in[m].astype(f32)).astype(bf)

    kx = {}
    kz = {}
    for i in (4, 3, 5, 2, 6, 1, 7):
        kz[i] = comm.send(part_z.at[(z + i) % 8], z_in.at[i - 1], peer(dz=i))
        if i in (1, 2, 3):
            kx[i] = comm.send(part_x.at[(x + i) % 4], x_in.at[i - 1], peer(dx=i))

    whole = fpad[1:9, 8:40, :].reshape(256, 256)
    ocean_out[...] = ((whole + oacc[...]) * wet[...]).astype(bf).reshape(8, 32, 256)
    comm.recv(kr[0], relay_in.at[0])
    relay_sum[0] = (part[(p + 3) % 4, :, 0:768].astype(f32) + relay_in[0].astype(f32)).astype(bf)
    ks = [comm.send(relay_sum.at[0], summed_in.at[0], down)]
    comm.recv(kr[1], relay_in.at[1])
    relay_sum[1] = (part[(p + 1) % 4, :, 768:1536].astype(f32) + relay_in[1].astype(f32)).astype(bf)
    ks.append(comm.send(relay_sum.at[1], summed_in.at[1], up))

    for i in (1, 3, 2):
        comm.recv(kx[i], x_in.at[i - 1])
    for n in range(8):
        acc = terms[x * 8 + n, c] + core_in[x * 8 + n].astype(f32)
        for i in range(3):
            acc = acc + x_in[i, n].astype(f32)
        sum0[n] = acc
        part_xz[n] = acc.astype(bf)
    kxz = {}
    for i in (4, 3, 5, 2, 6, 1, 7):
        kxz[i] = comm.send(part_xz.at[(z + i) % 8], xz_in.at[i - 1], peer(dz=i))
    for i in (1, 7, 2, 6, 3, 5, 4):
        comm.recv(kz[i], z_in.at[i - 1])
    for n in range(4):
        m = 32 + n * 8 + z
        acc = terms[m, c] + core_in[m].astype(f32)
        for i in range(7):
            acc = acc + z_in[i, n].astype(f32)
        sum0[8 + n] = acc
        part_zx[n] = acc.astype(bf)
    kzx = {}
    for i in (2, 1, 3):
        kzx[i] = comm.send(part_zx.at[(x + i) % 4], zx_in.at[i - 1], peer(dx=i))
    for i in (1, 7, 2, 6, 3, 5, 4):
        comm.recv(kxz[i], xz_in.at[i - 1])
    acc = sum0[z]
    for i in range(7):
        acc = acc + xz_in[i].astype(f32)
    for q in range(4):
        part_y[2 * q, 0:4, :] = acc[4 * q : 4 * q + 4, :]
        part_y[2 * q, 4:8, :] = jnp.zeros((4, 256), f32)
    for i in (1, 3, 2):
        comm.recv(kzx[i], zx_in.at[i - 1])
    acc = sum0[8 + x]
    for i in range(3):
        acc = acc + zx_in[i].astype(f32)
    for q in range(4):
        part_y[2 * q + 1, 0:4, :] = acc[4 * q : 4 * q + 4, :]
        part_y[2 * q + 1, 4:8, :] = jnp.zeros((4, 256), f32)
    ky = {}
    for i in (4, 3, 5, 2, 6, 1, 7):
        ky[i] = comm.send(part_y.at[(y + i) % 8], y_in.at[i - 1], peer(dy=i))
    acc = part_y[y]
    for i in (1, 7, 2, 6, 3, 5, 4):
        comm.recv(ky[i], y_in.at[i - 1])
        acc = acc + y_in[i - 1]
    grads_out[...] = acc[0:4, :]

    for n in range(2):
        comm.recv(kd[n], direct_in.at[n])
        comm.recv(ks[n], summed_in.at[n])

    @pl.loop(0, 8)
    def _(n):
        at = pl.ds(pl.multiple_of(n * 16, 16), 16)
        own_rows = state[pl.ds(pl.multiple_of(p * 128 + n * 16, 16), 16), :].astype(f32)
        for h in range(2):
            cols = slice(768 * h, 768 * h + 768)
            acc = part[p, at, cols].astype(f32) + direct_in[h, at, :].astype(f32)
            acc = acc + summed_in[h, at, :].astype(f32)
            atmos_out[at, cols] = (own_rows[:, cols] + acc).astype(bf)

    comm.drain()


def vmem(shape, dtype):
    return pltpu.VMEM(shape, dtype)


WHOLE = pl.BlockSpec(memory_space=pltpu.VMEM)
ANY = pl.BlockSpec(memory_space=pl.ANY)


def write_out(a, b, c, a_out, b_out, c_out, sems):
    copies = [
        pltpu.make_async_copy(src, dst, sems.at[n])
        for n, (src, dst) in enumerate(((a, a_out), (b, b_out), (c, c_out)))
    ]
    for copy in copies:
        copy.start()
    for copy in copies:
        copy.wait()


def on_device(
    atmos_state,
    atmos_gain,
    w_first,
    w_second,
    flux_proj,
    remap_index,
    remap_weight,
    ocean_state,
    depth_levels,
    conv_kernel,
    ocean_gain,
    ocean_w_in,
    ocean_w_out,
    ocean_cotangent,
):
    bf = jnp.bfloat16
    f32 = jnp.float32
    copies = 192
    big = (
        w_first, w_second, atmos_state, flux_proj, remap_weight, ocean_state, ocean_cotangent,
        ocean_w_in, ocean_w_out,
    )
    shapes = (
        jax.ShapeDtypeStruct((128, 1536), bf),
        jax.ShapeDtypeStruct((8, 32, 256), bf),
        jax.ShapeDtypeStruct((4, 256), f32),
    )
    results = pl.pallas_call(
        kernel,
        out_shape=shapes,
        in_specs=[ANY] * 9
        + [WHOLE] * 4
        + [pl.BlockSpec(memory_space=pltpu.SMEM)],
        out_specs=(WHOLE, WHOLE, WHOLE),
        scratch_shapes=[vmem(a.shape, a.dtype) for a in (w_first, w_second, atmos_state, flux_proj)]
        + [vmem(a.shape, a.dtype) for a in big[4:]]
        + [
            vmem((4, 2, 16, 768), bf),
            vmem((2, 48, 384), f32),
            vmem((4, 8, 48, 768), bf),
            vmem((4, 8, 48, 768), bf),
            vmem((1536, 768), bf),
            vmem((1536, 768), bf),
            vmem((512, 1536), bf),
            vmem((512, 768), bf),
            vmem((4, 128, 1536), bf),
            vmem((256, 1536), bf),
            vmem((256, 768), bf),
            vmem((4, 128, 256), f32),
            vmem((7, 128, 256), bf),
            vmem((4, 128, 256), bf),
            vmem((2, 128, 768), bf),
            vmem((2, 128, 768), bf),
            vmem((2, 128, 768), bf),
            vmem((2, 128, 768), bf),
            vmem((256, 256), f32),
            vmem((256, 256), bf),
            vmem((256, 1024), f32),
            vmem((10, 48, 256), f32),
            vmem((2, 8, 256), f32),
            vmem((2, 8, 256), f32),
            vmem((4, 8, 256), f32),
            vmem((256, 256), bf),
            vmem((256, 256), f32),
            vmem((64, 2, 16, 256), f32),
            vmem((2, 64, 16, 256), bf),
            vmem((64, 16, 256), bf),
            vmem((12, 16, 256), f32),
            vmem((4, 8, 16, 256), bf),
            vmem((8, 4, 16, 256), bf),
            vmem((3, 8, 16, 256), bf),
            vmem((7, 4, 16, 256), bf),
            vmem((8, 16, 256), bf),
            vmem((4, 16, 256), bf),
            vmem((7, 16, 256), bf),
            vmem((3, 16, 256), bf),
            vmem((8, 8, 256), f32),
            vmem((7, 8, 256), f32),
            pltpu.SemaphoreType.DMA((9,)),
            pltpu.SemaphoreType.DMA((copies,)),
            pltpu.SemaphoreType.DMA((copies,)),
        ],
        compiler_params=pltpu.CompilerParams(
            collective_id=0, has_side_effects=True, vmem_limit_bytes=56 << 20
        ),
        name="step",
    )(*big, atmos_gain, depth_levels, conv_kernel, ocean_gain, remap_index)
    return pl.pallas_call(
        write_out,
        out_shape=shapes,
        in_specs=[ANY] * 3,
        out_specs=(ANY, ANY, ANY),
        scratch_shapes=[pltpu.SemaphoreType.DMA((3,))],
        name="write_out",
    )(*results)


def solution(mesh):
    in_specs = (
        P(("grp", "tile"), None),
        P(),
        P(("grp", "tile"), "tp"),
        P(("grp", "tile"), "tp"),
        P(),
        P(("grp", "tile", "tp"), None),
        P(("grp", "tile", "tp"), None, None, None),
        P(("grp", "tile"), "tp", None),
        P(("grp", "tile"), "tp"),
        P(),
        P(),
        P(),
        P(),
        P(("grp", "tile"), "tp", None),
    )
    out_specs = (
        P(("grp", "tile", "tp"), None),
        P(("grp", "tile"), "tp", None),
        P(("grp", "tile", "tp"), None),
    )
    return jax.shard_map(
        on_device, mesh=mesh, in_specs=in_specs, out_specs=out_specs, check_vma=False
    )
```

time: 164 us -> 119 us (0.73)
  Pallas kernels: 133 us -> 116 us
  starting transfers between devices: 10 us -> 0 us
  waiting for transfers between devices: 6.9 us -> 0 us
  local copies, waits for them, and re-layouts: 6.34 us -> 0 us
  matrix products: 4.69 us -> 0 us
    pallas_call x2, Pallas kernels: 133 us -> 116 us  [the longest x1 99.3 us: on_device(): pl.pallas_call(kernel, out_shape=shapes, in_specs=[ANY] * 9 + [WHOLE] * 4...]
    ppermute x4 -> x0, starting transfers between devices: 10 us -> none  [the longest x2 6.82 us: with_halo(): lax.ppermute(lax.slice_in_dim(block, block.shape[dim] - width, None, axis...]
    ppermute x4 -> x0, waiting for transfers between devices: 6.9 us -> none  [the longest x2 6.89 us: with_halo(): lax.ppermute(lax.slice_in_dim(block, 0, width, axis=dim), axis, backward)]
    unnamed x30 -> x0, local copies, waits for them, and re-layouts: 5.49 us -> none
    dot_general x6 -> x0, matrix products: 4.69 us -> none  [the longest x1 2.09 us: on_device(): lax.dot_general(dpre, ocean_normed, (((0,), (0,)), ((), ())), preferred_e...]
  transfers between devices with their start and end apart: 4 -> 0, of which waited for: 2 -> 0; matrix products, arithmetic and copies ran while one was open for 0% -> 0% of each run, Pallas kernels for 0% -> 0%
where the time goes in v2:
time: 119 us; the launch traced here: 117 us
  Pallas kernels  116 us (97%)
    pallas_call x1, Pallas kernels, on_device(): pl.pallas_call(kernel, out_shape=shapes, in_specs=[ANY] * 9 + [WHOLE] * 4...  99.3 us
    pallas_call x1, Pallas kernels, on_device(): pl.pallas_call(write_out, out_shape=shapes, in_specs=[ANY] * 3, out_specs...  17.1 us

profile of v2, /device:TPU:1, one launch (start us, length us, event | category | flops | bytes accessed | tf_op | source)
XLA Modules:
  0.0 117.1 jit_solution(7025584261663232037)
XLA Ops:
  0.6 99.3 %step.1 = (bf16[128,1536]{1,0:T(8,128)(2,1)}, bf16[8,32,256]{2,1,0:T(8,128)(2,1)}, f32[4,256]{1,0:T(4,128)}) custom-call(bf16[12,768]{1,0:T(8,128)(2,1)} %w1_hbm.1, bf16[12,768]{1,0:T(8,128)(2,1)} %w2_hbm.1, bf16[512,1536]{1,0:T(8,128)(2,1)} %state_hbm.1, bf16[1536,256]{1,0:T(8,128)(2,1)} %proj_hbm.1, bf16[2,3,128,128]{3,2,1,0:T(8,128)(2,1)} %remap_hbm.1, ...), custom_call_target="tpu_custom_call" | custom-call | tf_op jit(solution)/shard_map/step/pallas_call | solution.py:581
  99.9 17.1 %write_out.1 = (bf16[128,1536]{1,0:T(8,128)(2,1)}, bf16[8,32,256]{2,1,0:T(8,128)(2,1)}, f32[4,256]{1,0:T(4,128)}) custom-call(bf16[128,1536]{1,0:T(8,128)(2,1)} %get-tuple-element.6.a, bf16[8,32,256]{2,1,0:T(8,128)(2,1)} %get-tuple-element.7.b, f32[4,256]{1,0:T(4,128)} %get-tuple-element.8.c), custom_call_target="tpu_custom_call" | custom-call | tf_op jit(solution)/shard_map/write_out/pallas_call | solution.py:641

commit v3 on v2

--- a/solution.py
+++ b/solution.py
@@ -93,7 +93,7 @@
     stage, compose, g1, g2, w1n, w2n, normed, hidden, part, proj_t, wf_t, fluxp, fluxin, flux_all,
     relay_in, relay_sum, direct_in, summed_in,
     wet, dout, dact, fpad, edge, edge_in, corner_in, onorm, oacc,
-    terms, out16, core_in, sum0, part_x, part_z, x_in, z_in, part_xz, part_zx, xz_in, zx_in,
+    terms, out16, core_in, sum_x, sum_z, part_x, part_z, x_in, z_in, part_xz, part_zx, xz_in, zx_in,
     part_y, y_in,
     local_sems, send_sems, recv_sems,
 ):
@@ -159,7 +159,8 @@
     def zi(i):
         return (z + i + 8) % 8
 
-    handed = []
+    handed_1 = []
+    handed_2 = []
     every = pl.ds(0, 48)
     low = pl.ds(0, 32)
     high = pl.ds(32, 16)
@@ -174,11 +175,11 @@
 
     def hand1(at):
         ref = g1.at[:, at, :, half]
-        handed.append((comm.send(ref, ref, peer(dc=1)), g1.at[:, at, :, other]))
+        handed_1.append((comm.send(ref, ref, peer(dc=1)), g1.at[:, at, :, other]))
 
     def hand2(at):
         ref = g2.at[at, :, :, half]
-        handed.append((comm.send(ref, ref, peer(dc=1)), g2.at[at, :, :, other]))
+        handed_2.append((comm.send(ref, ref, peer(dc=1)), g2.at[at, :, :, other]))
 
     k2z = {}
     k1x = {}
@@ -272,9 +273,6 @@
         if later_2x:
             round_2x(*later_2x.pop(0))
 
-    for k, ref in handed:
-        comm.recv(k, ref)
-
     def in_order(src, dst):
         @pl.loop(0, 16)
         def _(j):
@@ -284,15 +282,24 @@
             dst[pl.ds(at, 48), :] = jnp.concatenate([a[:24], b[:24]], axis=0).astype(bf)
             dst[pl.ds(768 + at, 48), :] = jnp.concatenate([a[24:], b[24:]], axis=0).astype(bf)
 
+    for k, ref in handed_2:
+        comm.recv(k, ref)
+    in_order(g2, w2n)
+
+    @pl.loop(0, 3)
+    def _(n):
+        at = pl.ds(pl.multiple_of(n * 256, 256), 256)
+        wf_t[:, at] = jnp.dot(proj_t[...], w2n[:, at], preferred_element_type=f32).astype(bf)
+
+    for k, ref in handed_1:
+        comm.recv(k, ref)
     in_order(g1, w1n)
-    in_order(g2, w2n)
 
     @pl.loop(0, 3)
     def _(n):
         at = pl.ds(pl.multiple_of(n * 256, 256), 256)
         pre = jnp.dot(normed[...], w1n[:, at], preferred_element_type=f32)
         hidden[:, at] = gelu(pre).astype(bf)
-        wf_t[:, at] = jnp.dot(proj_t[...], w2n[:, at], preferred_element_type=f32).astype(bf)
 
     for q in range(4):
         fp = lax.dot_general(
@@ -322,6 +329,15 @@
     kg = {}
     for i in (2, 1, 3):
         kg[i] = comm.send(flux_all.at[p], flux_all.at[p], peer(dy=2 * i))
+
+    left_cols = pl.ds(0, 768)
+    right_cols = pl.ds(768, 768)
+    up = peer(dy=2)
+    down = peer(dy=6)
+    kr = [
+        comm.send(part.at[(p + 2) % 4, :, left_cols], relay_in.at[0], down),
+        comm.send(part.at[(p + 2) % 4, :, right_cols], relay_in.at[1], up),
+    ]
 
     for load in loads[4:]:
         load.wait()
@@ -369,14 +385,6 @@
         comm.send(edge.at[1], corner_in.at[3], near(-1, 1)),
     ]
 
-    left_cols = pl.ds(0, 768)
-    right_cols = pl.ds(768, 768)
-    up = peer(dy=2)
-    down = peer(dy=6)
-    kr = [
-        comm.send(part.at[(p + 2) % 4, :, left_cols], relay_in.at[0], down),
-        comm.send(part.at[(p + 2) % 4, :, right_cols], relay_in.at[1], up),
-    ]
     kd = [
         comm.send(part.at[(p + 1) % 4, :, left_cols], direct_in.at[0], up),
         comm.send(part.at[(p + 3) % 4, :, right_cols], direct_in.at[1], down),
@@ -441,14 +449,26 @@
         else:
             oacc[...] += more
 
-    for k, ref in kcore:
-        comm.recv(k, ref)
-
-    @pl.loop(0, 32)
-    def _(n):
-        part_x[n // 8, n % 8] = (terms[n, c] + core_in[n].astype(f32)).astype(bf)
-        m = n + 32
-        part_z[n % 8, n // 8] = (terms[m, c] + core_in[m].astype(f32)).astype(bf)
+    comm.recv(kr[0], relay_in.at[0])
+    relay_sum[0] = (part[(p + 3) % 4, :, 0:768].astype(f32) + relay_in[0].astype(f32)).astype(bf)
+    ks = [comm.send(relay_sum.at[0], summed_in.at[0], down)]
+    comm.recv(kr[1], relay_in.at[1])
+    relay_sum[1] = (part[(p + 1) % 4, :, 768:1536].astype(f32) + relay_in[1].astype(f32)).astype(bf)
+    ks.append(comm.send(relay_sum.at[1], summed_in.at[1], up))
+
+    def own_sum(m):
+        return terms[m, c] + core_in[m].astype(f32)
+
+    for n in range(4):
+        for k, ref in kcore[2 * n : 2 * n + 2]:
+            comm.recv(k, ref)
+
+        @pl.loop(0, 8)
+        def _(m):
+            part_x[n, m, :, 0:256] = own_sum(8 * n + m).astype(bf)
+            second = own_sum(32 + 8 * n + m).astype(bf)
+            part_x[n, m, :, 256:384] = second[:, 0:128]
+            part_z[m, n] = second[:, 128:256]
 
     kx = {}
     kz = {}
@@ -459,20 +479,13 @@
 
     whole = fpad[1:9, 8:40, :].reshape(256, 256)
     ocean_out[...] = ((whole + oacc[...]) * wet[...]).astype(bf).reshape(8, 32, 256)
-    comm.recv(kr[0], relay_in.at[0])
-    relay_sum[0] = (part[(p + 3) % 4, :, 0:768].astype(f32) + relay_in[0].astype(f32)).astype(bf)
-    ks = [comm.send(relay_sum.at[0], summed_in.at[0], down)]
-    comm.recv(kr[1], relay_in.at[1])
-    relay_sum[1] = (part[(p + 1) % 4, :, 768:1536].astype(f32) + relay_in[1].astype(f32)).astype(bf)
-    ks.append(comm.send(relay_sum.at[1], summed_in.at[1], up))
-
     for i in (1, 3, 2):
         comm.recv(kx[i], x_in.at[i - 1])
     for n in range(8):
-        acc = terms[x * 8 + n, c] + core_in[x * 8 + n].astype(f32)
+        acc = jnp.concatenate([own_sum(x * 8 + n), own_sum(32 + x * 8 + n)[:, 0:128]], axis=1)
         for i in range(3):
             acc = acc + x_in[i, n].astype(f32)
-        sum0[n] = acc
+        sum_x[n] = acc
         part_xz[n] = acc.astype(bf)
     kxz = {}
     for i in (4, 3, 5, 2, 6, 1, 7):
@@ -480,30 +493,30 @@
     for i in (1, 7, 2, 6, 3, 5, 4):
         comm.recv(kz[i], z_in.at[i - 1])
     for n in range(4):
-        m = 32 + n * 8 + z
-        acc = terms[m, c] + core_in[m].astype(f32)
+        acc = own_sum(32 + n * 8 + z)[:, 128:256]
         for i in range(7):
             acc = acc + z_in[i, n].astype(f32)
-        sum0[8 + n] = acc
+        sum_z[n] = acc
         part_zx[n] = acc.astype(bf)
     kzx = {}
     for i in (2, 1, 3):
         kzx[i] = comm.send(part_zx.at[(x + i) % 4], zx_in.at[i - 1], peer(dx=i))
     for i in (1, 7, 2, 6, 3, 5, 4):
         comm.recv(kxz[i], xz_in.at[i - 1])
-    acc = sum0[z]
+    acc = sum_x[z]
     for i in range(7):
         acc = acc + xz_in[i].astype(f32)
     for q in range(4):
-        part_y[2 * q, 0:4, :] = acc[4 * q : 4 * q + 4, :]
+        part_y[2 * q, 0:4, :] = acc[4 * q : 4 * q + 4, 0:256]
         part_y[2 * q, 4:8, :] = jnp.zeros((4, 256), f32)
+        part_y[2 * q + 1, 0:4, 0:128] = acc[4 * q : 4 * q + 4, 256:384]
     for i in (1, 3, 2):
         comm.recv(kzx[i], zx_in.at[i - 1])
-    acc = sum0[8 + x]
+    acc = sum_z[x]
     for i in range(3):
         acc = acc + zx_in[i].astype(f32)
     for q in range(4):
-        part_y[2 * q + 1, 0:4, :] = acc[4 * q : 4 * q + 4, :]
+        part_y[2 * q + 1, 0:4, 128:256] = acc[4 * q : 4 * q + 4, :]
         part_y[2 * q + 1, 4:8, :] = jnp.zeros((4, 256), f32)
     ky = {}
     for i in (4, 3, 5, 2, 6, 1, 7):
@@ -618,15 +631,16 @@
             vmem((64, 2, 16, 256), f32),
             vmem((2, 64, 16, 256), bf),
             vmem((64, 16, 256), bf),
-            vmem((12, 16, 256), f32),
-            vmem((4, 8, 16, 256), bf),
-            vmem((8, 4, 16, 256), bf),
-            vmem((3, 8, 16, 256), bf),
-            vmem((7, 4, 16, 256), bf),
-            vmem((8, 16, 256), bf),
-            vmem((4, 16, 256), bf),
-            vmem((7, 16, 256), bf),
-            vmem((3, 16, 256), bf),
+            vmem((8, 16, 384), f32),
+            vmem((4, 16, 128), f32),
+            vmem((4, 8, 16, 384), bf),
+            vmem((8, 4, 16, 128), bf),
+            vmem((3, 8, 16, 384), bf),
+            vmem((7, 4, 16, 128), bf),
+            vmem((8, 16, 384), bf),
+            vmem((4, 16, 128), bf),
+            vmem((7, 16, 384), bf),
+            vmem((3, 16, 128), bf),
             vmem((8, 8, 256), f32),
             vmem((7, 8, 256), f32),
             pltpu.SemaphoreType.DMA((9,)),
@@ -641,7 +655,7 @@
     return pl.pallas_call(
         write_out,
         out_shape=shapes,
-        in_specs=[ANY] * 3,
+        in_specs=[WHOLE] * 3,
         out_specs=(ANY, ANY, ANY),
         scratch_shapes=[pltpu.SemaphoreType.DMA((3,))],
         name="write_out",

time: 119 us -> 108 us (0.908)
  Pallas kernels: 116 us -> 106 us
    pallas_call x1, Pallas kernels: 17.1 us -> 1.88 us  [on_device(): pl.pallas_call(write_out, out_shape=shapes, in_specs=[WHOLE] * 3, out_spe...]
    pallas_call x1, Pallas kernels: 99.3 us -> 104 us  [on_device(): pl.pallas_call(kernel, out_shape=shapes, in_specs=[ANY] * 9 + [WHOLE] * 4...]
where the time goes in v3:
time: 108 us; the launch traced here: 107 us
  Pallas kernels  106 us (98%)
    pallas_call x1, Pallas kernels, on_device(): pl.pallas_call(kernel, out_shape=shapes, in_specs=[ANY] * 9 + [WHOLE] * 4...  104 us

profile of v3, /device:TPU:1, one launch (start us, length us, event | category | flops | bytes accessed | tf_op | source)
XLA Modules:
  0.0 106.6 jit_solution(1453066522038439918)
XLA Ops:
  0.6 104.1 %step.1 = (bf16[128,1536]{1,0:T(8,128)(2,1)}, bf16[8,32,256]{2,1,0:T(8,128)(2,1)}, f32[4,256]{1,0:T(4,128)}) custom-call(bf16[12,768]{1,0:T(8,128)(2,1)} %w1_hbm.1, bf16[12,768]{1,0:T(8,128)(2,1)} %w2_hbm.1, bf16[512,1536]{1,0:T(8,128)(2,1)} %state_hbm.1, bf16[1536,256]{1,0:T(8,128)(2,1)} %proj_hbm.1, bf16[2,3,128,128]{3,2,1,0:T(8,128)(2,1)} %remap_hbm.1, ...), custom_call_target="tpu_custom_call" | custom-call | tf_op jit(solution)/shard_map/step/pallas_call | solution.py:594
  104.7 1.9 %write_out.1 = (bf16[128,1536]{1,0:T(8,128)(2,1)}, bf16[8,32,256]{2,1,0:T(8,128)(2,1)}, f32[4,256]{1,0:T(4,128)}) custom-call(bf16[128,1536]{1,0:T(8,128)(2,1)} %get-tuple-element.6.a, bf16[8,32,256]{2,1,0:T(8,128)(2,1)} %get-tuple-element.7.b, f32[4,256]{1,0:T(4,128)} %get-tuple-element.8.c), custom_call_target="tpu_custom_call" | custom-call | tf_op jit(solution)/shard_map/write_out/pallas_call | solution.py:655

commit v4 on v3

--- a/solution.py
+++ b/solution.py
@@ -123,10 +123,6 @@
     loads[1].wait()
     stage[slot, 0, 0:12, :] = w1[...]
     stage[slot, 1, 0:12, :] = w2[...]
-    loads[2].wait()
-    for n in range(6):
-        at = slice(256 * n, 256 * n + 256)
-        proj_t[:, at] = proj[at, :].astype(f32).T.astype(bf)
     pl.semaphore_wait(entry, len(peers))
 
     own = stage.at[slot]
@@ -142,6 +138,11 @@
         wide = state[at, :].astype(f32)
         scale = lax.rsqrt(jnp.mean(wide * wide, axis=-1, keepdims=True) + epsilon)
         normed[at, :] = (wide * scale * gain[...]).astype(bf)
+
+    loads[2].wait()
+    for n in range(6):
+        at = slice(256 * n, 256 * n + 256)
+        proj_t[:, at] = proj[at, :].astype(f32).T.astype(bf)
 
     half = pl.ds(pl.multiple_of(c * 384, 128), 384)
     other = pl.ds(pl.multiple_of((1 - c) * 384, 128), 384)
@@ -329,15 +330,6 @@
     kg = {}
     for i in (2, 1, 3):
         kg[i] = comm.send(flux_all.at[p], flux_all.at[p], peer(dy=2 * i))
-
-    left_cols = pl.ds(0, 768)
-    right_cols = pl.ds(768, 768)
-    up = peer(dy=2)
-    down = peer(dy=6)
-    kr = [
-        comm.send(part.at[(p + 2) % 4, :, left_cols], relay_in.at[0], down),
-        comm.send(part.at[(p + 2) % 4, :, right_cols], relay_in.at[1], up),
-    ]
 
     for load in loads[4:]:
         load.wait()
@@ -385,6 +377,14 @@
         comm.send(edge.at[1], corner_in.at[3], near(-1, 1)),
     ]
 
+    left_cols = pl.ds(0, 768)
+    right_cols = pl.ds(768, 768)
+    up = peer(dy=2)
+    down = peer(dy=6)
+    kr = [
+        comm.send(part.at[(p + 2) % 4, :, left_cols], relay_in.at[0], down),
+        comm.send(part.at[(p + 2) % 4, :, right_cols], relay_in.at[1], up),
+    ]
     kd = [
         comm.send(part.at[(p + 1) % 4, :, left_cols], direct_in.at[0], up),
         comm.send(part.at[(p + 3) % 4, :, right_cols], direct_in.at[1], down),

time: 108 us -> 107 us (level); the launches traced: 107 us -> 107 us
  no operation moved by 1% of the time
where the time goes in v4:
time: 107 us
  Pallas kernels  106 us (99%)
    pallas_call x1, Pallas kernels, on_device(): pl.pallas_call(kernel, out_shape=shapes, in_specs=[ANY] * 9 + [WHOLE] * 4...  105 us

profile of v4, /device:TPU:1, one launch (start us, length us, event | category | flops | bytes accessed | tf_op | source)
XLA Modules:
  0.0 107.0 jit_solution(18374171544065292229)
XLA Ops:
  0.6 104.5 %step.1 = (bf16[128,1536]{1,0:T(8,128)(2,1)}, bf16[8,32,256]{2,1,0:T(8,128)(2,1)}, f32[4,256]{1,0:T(4,128)}) custom-call(bf16[12,768]{1,0:T(8,128)(2,1)} %w1_hbm.1, bf16[12,768]{1,0:T(8,128)(2,1)} %w2_hbm.1, bf16[512,1536]{1,0:T(8,128)(2,1)} %state_hbm.1, bf16[1536,256]{1,0:T(8,128)(2,1)} %proj_hbm.1, bf16[2,3,128,128]{3,2,1,0:T(8,128)(2,1)} %remap_hbm.1, ...), custom_call_target="tpu_custom_call" | custom-call | tf_op jit(solution)/shard_map/step/pallas_call | solution.py:594
  105.2 1.9 %write_out.1 = (bf16[128,1536]{1,0:T(8,128)(2,1)}, bf16[8,32,256]{2,1,0:T(8,128)(2,1)}, f32[4,256]{1,0:T(4,128)}) custom-call(bf16[128,1536]{1,0:T(8,128)(2,1)} %get-tuple-element.6.a, bf16[8,32,256]{2,1,0:T(8,128)(2,1)} %get-tuple-element.7.b, f32[4,256]{1,0:T(4,128)} %get-tuple-element.8.c), custom_call_target="tpu_custom_call" | custom-call | tf_op jit(solution)/shard_map/write_out/pallas_call | solution.py:655

commit v5 on v4

--- a/solution.py
+++ b/solution.py
@@ -349,8 +349,18 @@
         dact[:, at] = lax.dot_general(
             dout[...], wout[at, :], (((1,), (1,)), ((), ())), preferred_element_type=f32
         )
-    for i in (1, 3, 2):
+    for i in (1, 3):
         comm.recv(kg[i], flux_all.at[(p - i + 4) % 4])
+
+    left_cols = pl.ds(0, 768)
+    right_cols = pl.ds(768, 768)
+    up = peer(dy=2)
+    down = peer(dy=6)
+    kr = [
+        comm.send(part.at[(p + 2) % 4, :, left_cols], relay_in.at[0], down),
+        comm.send(part.at[(p + 2) % 4, :, right_cols], relay_in.at[1], up),
+    ]
+    comm.recv(kg[2], flux_all.at[(p + 2) % 4])
 
     for b in range(2):
         acc = jnp.zeros((128, 256), f32)
@@ -377,14 +387,6 @@
         comm.send(edge.at[1], corner_in.at[3], near(-1, 1)),
     ]
 
-    left_cols = pl.ds(0, 768)
-    right_cols = pl.ds(768, 768)
-    up = peer(dy=2)
-    down = peer(dy=6)
-    kr = [
-        comm.send(part.at[(p + 2) % 4, :, left_cols], relay_in.at[0], down),
-        comm.send(part.at[(p + 2) % 4, :, right_cols], relay_in.at[1], up),
-    ]
     kd = [
         comm.send(part.at[(p + 1) % 4, :, left_cols], direct_in.at[0], up),
         comm.send(part.at[(p + 3) % 4, :, right_cols], direct_in.at[1], down),

time: 107 us -> 108 us (level); the launches traced: 107 us -> 107 us
  no operation moved by 1% of the time
where the time goes in v5:
time: 108 us; the launch traced here: 107 us
  Pallas kernels  106 us (98%)
    pallas_call x1, Pallas kernels, on_device(): pl.pallas_call(kernel, out_shape=shapes, in_specs=[ANY] * 9 + [WHOLE] * 4...  104 us

profile of v5, /device:TPU:1, one launch (start us, length us, event | category | flops | bytes accessed | tf_op | source)
XLA Modules:
  0.0 106.7 jit_solution(17648260763003092922)
XLA Ops:
  0.6 104.2 %step.1 = (bf16[128,1536]{1,0:T(8,128)(2,1)}, bf16[8,32,256]{2,1,0:T(8,128)(2,1)}, f32[4,256]{1,0:T(4,128)}) custom-call(bf16[12,768]{1,0:T(8,128)(2,1)} %w1_hbm.1, bf16[12,768]{1,0:T(8,128)(2,1)} %w2_hbm.1, bf16[512,1536]{1,0:T(8,128)(2,1)} %state_hbm.1, bf16[1536,256]{1,0:T(8,128)(2,1)} %proj_hbm.1, bf16[2,3,128,128]{3,2,1,0:T(8,128)(2,1)} %remap_hbm.1, ...), custom_call_target="tpu_custom_call" | custom-call | tf_op jit(solution)/shard_map/step/pallas_call | solution.py:596
  104.8 1.9 %write_out.1 = (bf16[128,1536]{1,0:T(8,128)(2,1)}, bf16[8,32,256]{2,1,0:T(8,128)(2,1)}, f32[4,256]{1,0:T(4,128)}) custom-call(bf16[128,1536]{1,0:T(8,128)(2,1)} %get-tuple-element.6.a, bf16[8,32,256]{2,1,0:T(8,128)(2,1)} %get-tuple-element.7.b, f32[4,256]{1,0:T(4,128)} %get-tuple-element.8.c), custom_call_target="tpu_custom_call" | custom-call | tf_op jit(solution)/shard_map/write_out/pallas_call | solution.py:657

commit v6 on v2

--- a/solution.py
+++ b/solution.py
@@ -159,7 +159,8 @@
     def zi(i):
         return (z + i + 8) % 8
 
-    handed = []
+    handed_1 = []
+    handed_2 = []
     every = pl.ds(0, 48)
     low = pl.ds(0, 32)
     high = pl.ds(32, 16)
@@ -174,11 +175,11 @@
 
     def hand1(at):
         ref = g1.at[:, at, :, half]
-        handed.append((comm.send(ref, ref, peer(dc=1)), g1.at[:, at, :, other]))
+        handed_1.append((comm.send(ref, ref, peer(dc=1)), g1.at[:, at, :, other]))
 
     def hand2(at):
         ref = g2.at[at, :, :, half]
-        handed.append((comm.send(ref, ref, peer(dc=1)), g2.at[at, :, :, other]))
+        handed_2.append((comm.send(ref, ref, peer(dc=1)), g2.at[at, :, :, other]))
 
     k2z = {}
     k1x = {}
@@ -272,9 +273,6 @@
         if later_2x:
             round_2x(*later_2x.pop(0))
 
-    for k, ref in handed:
-        comm.recv(k, ref)
-
     def in_order(src, dst):
         @pl.loop(0, 16)
         def _(j):
@@ -284,15 +282,24 @@
             dst[pl.ds(at, 48), :] = jnp.concatenate([a[:24], b[:24]], axis=0).astype(bf)
             dst[pl.ds(768 + at, 48), :] = jnp.concatenate([a[24:], b[24:]], axis=0).astype(bf)
 
+    for k, ref in handed_2:
+        comm.recv(k, ref)
+    in_order(g2, w2n)
+
+    @pl.loop(0, 3)
+    def _(n):
+        at = pl.ds(pl.multiple_of(n * 256, 256), 256)
+        wf_t[:, at] = jnp.dot(proj_t[...], w2n[:, at], preferred_element_type=f32).astype(bf)
+
+    for k, ref in handed_1:
+        comm.recv(k, ref)
     in_order(g1, w1n)
-    in_order(g2, w2n)
 
     @pl.loop(0, 3)
     def _(n):
         at = pl.ds(pl.multiple_of(n * 256, 256), 256)
         pre = jnp.dot(normed[...], w1n[:, at], preferred_element_type=f32)
         hidden[:, at] = gelu(pre).astype(bf)
-        wf_t[:, at] = jnp.dot(proj_t[...], w2n[:, at], preferred_element_type=f32).astype(bf)
 
     for q in range(4):
         fp = lax.dot_general(
@@ -641,7 +648,7 @@
     return pl.pallas_call(
         write_out,
         out_shape=shapes,
-        in_specs=[ANY] * 3,
+        in_specs=[WHOLE] * 3,
         out_specs=(ANY, ANY, ANY),
         scratch_shapes=[pltpu.SemaphoreType.DMA((3,))],
         name="write_out",

time: 119 us -> 104 us (0.87)
  Pallas kernels: 116 us -> 102 us
    pallas_call x1, Pallas kernels: 17.1 us -> 1.88 us  [on_device(): pl.pallas_call(write_out, out_shape=shapes, in_specs=[WHOLE] * 3, out_spe...]
    pallas_call x1, Pallas kernels: 99.3 us -> 101 us  [on_device(): pl.pallas_call(kernel, out_shape=shapes, in_specs=[ANY] * 9 + [WHOLE] * 4...]
where the time goes in v6:
time: 104 us; the launch traced here: 103 us
  Pallas kernels  102 us (98%)
    pallas_call x1, Pallas kernels, on_device(): pl.pallas_call(kernel, out_shape=shapes, in_specs=[ANY] * 9 + [WHOLE] * 4...  101 us

profile of v6, /device:TPU:1, one launch (start us, length us, event | category | flops | bytes accessed | tf_op | source)
XLA Modules:
  0.0 103.1 jit_solution(13536286737982436422)
XLA Ops:
  0.6 100.5 %step.1 = (bf16[128,1536]{1,0:T(8,128)(2,1)}, bf16[8,32,256]{2,1,0:T(8,128)(2,1)}, f32[4,256]{1,0:T(4,128)}) custom-call(bf16[12,768]{1,0:T(8,128)(2,1)} %w1_hbm.1, bf16[12,768]{1,0:T(8,128)(2,1)} %w2_hbm.1, bf16[512,1536]{1,0:T(8,128)(2,1)} %state_hbm.1, bf16[1536,256]{1,0:T(8,128)(2,1)} %proj_hbm.1, bf16[2,3,128,128]{3,2,1,0:T(8,128)(2,1)} %remap_hbm.1, ...), custom_call_target="tpu_custom_call" | custom-call | tf_op jit(solution)/shard_map/step/pallas_call | solution.py:588
  101.2 1.9 %write_out.1 = (bf16[128,1536]{1,0:T(8,128)(2,1)}, bf16[8,32,256]{2,1,0:T(8,128)(2,1)}, f32[4,256]{1,0:T(4,128)}) custom-call(bf16[128,1536]{1,0:T(8,128)(2,1)} %get-tuple-element.6.a, bf16[8,32,256]{2,1,0:T(8,128)(2,1)} %get-tuple-element.7.b, f32[4,256]{1,0:T(4,128)} %get-tuple-element.8.c), custom_call_target="tpu_custom_call" | custom-call | tf_op jit(solution)/shard_map/write_out/pallas_call | solution.py:648

commit v7 on v6

--- a/solution.py
+++ b/solution.py
@@ -94,7 +94,7 @@
     relay_in, relay_sum, direct_in, summed_in,
     wet, dout, dact, fpad, edge, edge_in, corner_in, onorm, oacc,
     terms, out16, core_in, sum0, part_x, part_z, x_in, z_in, part_xz, part_zx, xz_in, zx_in,
-    part_y, y_in,
+    part_y, y_in, early,
     local_sems, send_sems, recv_sems,
 ):
     bf = jnp.bfloat16
@@ -123,10 +123,6 @@
     loads[1].wait()
     stage[slot, 0, 0:12, :] = w1[...]
     stage[slot, 1, 0:12, :] = w2[...]
-    loads[2].wait()
-    for n in range(6):
-        at = slice(256 * n, 256 * n + 256)
-        proj_t[:, at] = proj[at, :].astype(f32).T.astype(bf)
     pl.semaphore_wait(entry, len(peers))
 
     own = stage.at[slot]
@@ -142,6 +138,11 @@
         wide = state[at, :].astype(f32)
         scale = lax.rsqrt(jnp.mean(wide * wide, axis=-1, keepdims=True) + epsilon)
         normed[at, :] = (wide * scale * gain[...]).astype(bf)
+
+    loads[2].wait()
+    for n in range(6):
+        at = slice(256 * n, 256 * n + 256)
+        proj_t[:, at] = proj[at, :].astype(f32).T.astype(bf)
 
     half = pl.ds(pl.multiple_of(c * 384, 128), 384)
     other = pl.ds(pl.multiple_of((1 - c) * 384, 128), 384)
@@ -515,15 +516,8 @@
     ky = {}
     for i in (4, 3, 5, 2, 6, 1, 7):
         ky[i] = comm.send(part_y.at[(y + i) % 8], y_in.at[i - 1], peer(dy=i))
-    acc = part_y[y]
-    for i in (1, 7, 2, 6, 3, 5, 4):
-        comm.recv(ky[i], y_in.at[i - 1])
-        acc = acc + y_in[i - 1]
-    grads_out[...] = acc[0:4, :]
-
     for n in range(2):
         comm.recv(kd[n], direct_in.at[n])
-        comm.recv(ks[n], summed_in.at[n])
 
     @pl.loop(0, 8)
     def _(n):
@@ -531,9 +525,24 @@
         own_rows = state[pl.ds(pl.multiple_of(p * 128 + n * 16, 16), 16), :].astype(f32)
         for h in range(2):
             cols = slice(768 * h, 768 * h + 768)
-            acc = part[p, at, cols].astype(f32) + direct_in[h, at, :].astype(f32)
-            acc = acc + summed_in[h, at, :].astype(f32)
-            atmos_out[at, cols] = (own_rows[:, cols] + acc).astype(bf)
+            rows_in = part[p, at, cols].astype(f32) + direct_in[h, at, :].astype(f32)
+            early[at, cols] = own_rows[:, cols] + rows_in
+
+    acc = part_y[y]
+    for i in (1, 7, 2, 6, 3, 5, 4):
+        comm.recv(ky[i], y_in.at[i - 1])
+        acc = acc + y_in[i - 1]
+    grads_out[...] = acc[0:4, :]
+
+    for h in range(2):
+        comm.recv(ks[h], summed_in.at[h])
+        cols = slice(768 * h, 768 * h + 768)
+
+        @pl.loop(0, 4)
+        def _(n):
+            at = pl.ds(pl.multiple_of(n * 32, 32), 32)
+            total_rows = early[at, cols] + summed_in[h, at, :].astype(f32)
+            atmos_out[at, cols] = total_rows.astype(bf)
 
     comm.drain()
 
@@ -636,6 +645,7 @@
             vmem((3, 16, 256), bf),
             vmem((8, 8, 256), f32),
             vmem((7, 8, 256), f32),
+            vmem((128, 1536), f32),
             pltpu.SemaphoreType.DMA((9,)),
             pltpu.SemaphoreType.DMA((copies,)),
             pltpu.SemaphoreType.DMA((copies,)),

time: 104 us -> 104 us (level)
  no operation moved by 1% of the time
where the time goes in v7:
time: 104 us; the launch traced here: 102 us
  Pallas kernels  102 us (98%)
    pallas_call x1, Pallas kernels, on_device(): pl.pallas_call(kernel, out_shape=shapes, in_specs=[ANY] * 9 + [WHOLE] * 4...  99.6 us

profile of v7, /device:TPU:1, one launch (start us, length us, event | category | flops | bytes accessed | tf_op | source)
XLA Modules:
  0.0 102.2 jit_solution(17080955111925371082)
XLA Ops:
  0.6 99.6 %step.1 = (bf16[128,1536]{1,0:T(8,128)(2,1)}, bf16[8,32,256]{2,1,0:T(8,128)(2,1)}, f32[4,256]{1,0:T(4,128)}) custom-call(bf16[12,768]{1,0:T(8,128)(2,1)} %w1_hbm.1, bf16[12,768]{1,0:T(8,128)(2,1)} %w2_hbm.1, bf16[512,1536]{1,0:T(8,128)(2,1)} %state_hbm.1, bf16[1536,256]{1,0:T(8,128)(2,1)} %proj_hbm.1, bf16[2,3,128,128]{3,2,1,0:T(8,128)(2,1)} %remap_hbm.1, ...), custom_call_target="tpu_custom_call" | custom-call | tf_op jit(solution)/shard_map/step/pallas_call | solution.py:597
  100.3 1.9 %write_out.1 = (bf16[128,1536]{1,0:T(8,128)(2,1)}, bf16[8,32,256]{2,1,0:T(8,128)(2,1)}, f32[4,256]{1,0:T(4,128)}) custom-call(bf16[128,1536]{1,0:T(8,128)(2,1)} %get-tuple-element.6.a, bf16[8,32,256]{2,1,0:T(8,128)(2,1)} %get-tuple-element.7.b, f32[4,256]{1,0:T(4,128)} %get-tuple-element.8.c), custom_call_target="tpu_custom_call" | custom-call | tf_op jit(solution)/shard_map/write_out/pallas_call | solution.py:658
